TPU v7x, 32 devices: a whole 2x2x4 slice. The times are simulated.
32 devices in a mesh: join: 16 (over z, y, x), view: 2 (over core).
Axes of the slice: x: 2, y: 2, z: 4, core: 2. Of those that a mesh axis runs over, the one named last changes fastest.
Arguments:
- estimate: float32 [64, 256, 256], P('join', 'view'), may hold values from 0.5 to 2
- views: bfloat16 [64, 6, 256, 256], P('join', None, 'view'), may hold values from 0.25 to 4
- owners: int32 [64, 6], P('join'), may hold values from 0 to 15, all different within a row; in each aligned block of 4 rows (0 to 3, 4 to 7, ...) at most 3 rows name the same one
- local_blocks: int32 [64, 6], P('join'), may hold values from 0 to 3, as said below
- psf: float32 [6, 33], replicated, may hold values from 0.05 to 1
Outputs:
- deconvolved: float32 [64, 256, 256], P('join', 'view')
Inputs may be any that keep to these rules, and one draw needn't show every extreme that they name: `owners`: each row names 6 different join indices; in the 4 rows of one join index no join index is named more than 3 times, and in every draw some join index is named exactly 3 times by some device's rows. `local_blocks`: in every draw one local block index, drawn from the seed and neither 0 nor 4 - 1, is named by no entry, so the estimate blocks with that index are imaged by no view; the other values all appear.
All inputs are finite; a program needn't handle non-finite values.
Results may differ from a plain program's by a relative error of at most 0.00065.
Values may be sent and summed in bfloat16 or wider, within the bound.
No kernel may reach another device: no remote copies, remote signals or barrier semaphores. Data moves between devices by JAX's collectives and lax.ppermute only.
A program may use at most 64 MiB of HBM per device.

v0:
```python
import jax
import jax.numpy as jnp
from jax import lax
from jax.sharding import PartitionSpec as P

H = 16
CAP = 3
ITERS = 2


def padded(block, sides, width):
    for axis, dim in sides:
        count = lax.axis_size(axis)
        forward = [(i, i + 1) for i in range(count - 1)]
        backward = [(target, source) for source, target in forward]
        low = lax.ppermute(
            lax.slice_in_dim(block, block.shape[dim] - width, None, axis=dim), axis, forward
        )
        high = lax.ppermute(lax.slice_in_dim(block, 0, width, axis=dim), axis, backward)
        block = jnp.concatenate([low, block, high], axis=dim)
    return block


def toeplitz(kernel, width, inner):
    taps = kernel.shape[-1]
    offset = jnp.arange(width)[:, None] - jnp.arange(inner)[None, :]
    inside = (offset >= 0) & (offset < taps)
    picked = jnp.take(kernel, jnp.clip(offset, 0, taps - 1), axis=1)
    return jnp.where(inside[None], picked, jnp.zeros_like(picked))


def select_rows(table, data):
    return jnp.einsum("sb,bjr->sjr", table, data, preferred_element_type=jnp.float32).astype(
        jnp.bfloat16
    )


def local(estimate, views, owners, local_blocks, psf):
    blocks, depth, lat_rows = estimate.shape
    nviews = views.shape[1]
    peer_count = lax.axis_size("join")
    slot_cap = CAP
    slots = peer_count * slot_cap
    entries = blocks * nviews
    extent = depth + 2 * H
    normed = psf / jnp.sum(psf, axis=1, keepdims=True)
    kernel = normed.astype(jnp.bfloat16)
    forward = toeplitz(kernel, extent, depth)
    mirror = toeplitz(kernel[:, ::-1], extent, depth)
    target = owners.reshape(-1)
    in_owner = local_blocks.reshape(-1)
    view_id = jnp.tile(jnp.arange(nviews, dtype=jnp.int32), blocks)
    dest_hits = (target[:, None] == jnp.arange(peer_count, dtype=jnp.int32)[None, :]).astype(
        jnp.int32
    )
    order_in = jnp.sum(jnp.cumsum(dest_hits, axis=0) * dest_hits, axis=1) - 1
    slot_of = target * slot_cap + order_in
    slot_table = (slot_of[:, None] == jnp.arange(slots, dtype=jnp.int32)[None, :]).astype(jnp.int32)
    send_local = jnp.sum(slot_table * (in_owner[:, None] + 1), axis=0) - 1
    send_view = jnp.sum(slot_table * (view_id[:, None] + 1), axis=0) - 1
    got_local, got_view = (
        lax.all_to_all(
            send_local.reshape(peer_count, slot_cap),
            "join",
            split_axis=0,
            concat_axis=0,
            tiled=True,
        ),
        lax.all_to_all(
            send_view.reshape(peer_count, slot_cap), "join", split_axis=0, concat_axis=0, tiled=True
        ),
    )
    got_local = got_local.reshape(-1)
    got_view = got_view.reshape(-1)
    local_onehot = got_local[:, None] == jnp.arange(blocks, dtype=jnp.int32)[None, :]
    local_pick = local_onehot.astype(jnp.bfloat16)
    owner_onehot = jnp.transpose(local_onehot).astype(jnp.float32)
    counts = jnp.sum(owner_onehot, axis=1)
    send_full = jnp.transpose(slot_table).astype(jnp.float32)
    slot_pick = slot_table.astype(jnp.bfloat16)
    current = estimate
    for sweep in range(ITERS):
        rounded = current.astype(jnp.bfloat16)
        extended = padded(rounded, (("view", 1),), H)
        reply_buf = select_rows(local_pick, extended)
        fetched = lax.all_to_all(
            reply_buf.reshape(peer_count, slot_cap, extent, lat_rows),
            "join",
            split_axis=0,
            concat_axis=0,
            tiled=True,
        )
        gathered = select_rows(slot_pick, fetched.reshape(slots, extent, lat_rows)).reshape(
            blocks, nviews, extent, lat_rows
        )
        blurred = jnp.einsum(
            "bvjr,vjz->bvzr", gathered, forward, preferred_element_type=jnp.float32
        )
        quotient = (views.astype(jnp.float32) / blurred).astype(jnp.bfloat16)
        quot_ext = padded(quotient, (("view", 2),), H)
        correction = jnp.einsum(
            "bvjr,vjz->bvzr", quot_ext, mirror, preferred_element_type=jnp.float32
        )
        corr_rows = correction.reshape(entries, depth, lat_rows)
        outgoing = jnp.einsum(
            "se,ezr->szr",
            send_full,
            corr_rows,
            precision=lax.Precision.HIGHEST,
            preferred_element_type=jnp.float32,
        )
        returned = lax.all_to_all(
            outgoing.reshape(peer_count, slot_cap, depth, lat_rows),
            "join",
            split_axis=0,
            concat_axis=0,
            tiled=True,
        )
        returned = returned.reshape(slots, depth, lat_rows)
        summed = jnp.einsum(
            "bs,szr->bzr",
            owner_onehot,
            returned,
            precision=lax.Precision.HIGHEST,
            preferred_element_type=jnp.float32,
        )
        factor = jnp.where(
            (counts > 0)[:, None, None], summed / jnp.maximum(counts, 1.0)[:, None, None], 1.0
        )
        current = current * factor
    return current


def solution(mesh):
    in_specs = (
        P("join", "view", None),
        P("join", None, "view", None),
        P("join", None),
        P("join", None),
        P(),
    )
    out_specs = P("join", "view", None)
    return jax.shard_map(local, mesh=mesh, in_specs=in_specs, out_specs=out_specs, check_vma=False)
```

profile of v0, /device:TPU:13, one launch (start us, length us, event | category | flops | bytes accessed | tf_op | source)
XLA Modules:
  0.0 650.1 jit_solution(12031270275863208705)
XLA Ops:
  0.0 1.4 copy.158
  1.4 1.3 collective-permute-start
  2.7 3.0 collective-permute-start.1
  5.8 0.8 reshape.130
  6.8 0.7 broadcast_add_fusion
  7.8 10.6 %all_to_all.26 = s32[16,1,3]{2,1,0:T(1,128)S(1)} all-to-all(s32[16,1,3]{2,1,0:T(1,128)S(1)} %bitcast.89), channel_id=1, replica_groups=mesh['join'=16,'view'=2] {'join'}, dimensions={0} | all-to-all | bytes 384 | tf_op jit(solution)/shard_map/all_to_all | solution.py:62
  18.4 0.5 broadcast.205
  18.9 0.7 reduce.3
  19.6 1.2 convolution_convert_fusion.1
  20.9 3.3 copy.93
  24.2 6.5 all-to-all-start.1
  31.1 72.2 %gather_fusion.1 = bf16[20480,6]{1,0:T(8,128)(2,1)} fusion(bf16[6,33]{0,1:T(8,128)(2,1)S(1)} %copy.90, s32[20480]{0:T(1024)S(1)} %bitcast_clamp_fusion), kind=kCustom, calls=%fused_computation.1.clone | custom fusion | bytes 573440 | tf_op jit(solution)/shard_map/jit(_take)/gather | solution.py:28
  103.3 4.2 copy.91
  107.5 11.5 %all-to-all-done.1 = bf16[16,3,160,256]{3,2,1,0:T(8,128)(2,1)} async-done(((bf16[16,3,160,256]{3,2,1,0:T(8,128)(2,1)}), bf16[16,3,160,256]{3,2,1,0:T(8,128)(2,1)}, u32[]{:S(2)}, u32[]{:S(2)}) %all-to-all-start.1) | async-done | bytes 3932192 | tf_op jit(solution)/shard_map/all_to_all | solution.py:86
  119.0 4.4 fusion.38
  123.4 0.5 copy.95
  123.8 1.0 copy-done.2
  124.8 0.7 fusion.8
  125.5 1.3 collective-permute-start.2
  126.8 3.6 collective-permute-start.3
  130.6 72.2 %gather_fusion = bf16[20480,6]{1,0:T(8,128)(2,1)} fusion(bf16[6,33]{0,1:T(8,128)(2,1)S(1)} %copy.87, s32[20480]{0:T(1024)S(1)} %bitcast_clamp_fusion), kind=kCustom, calls=%fused_computation.clone | custom fusion | bytes 573440 | tf_op jit(solution)/shard_map/jit(_take)/gather | solution.py:28
  202.8 4.2 copy.88
  207.0 0.6 fusion.35
  208.0 7.3 %fusion.12 = f32[16,3,128,256]{3,0,2,1:T(8,128)S(1)} fusion(f32[24,128,256]{2,1,0:T(8,128)S(1)} %bitcast.84, s32[16,3]{0,1:T(4,128)S(1)} %multiply_add_fusion, s32[24]{0:T(128)S(1)} %add_add_fusion), kind=kOutput, calls=%fused_computation.16 | convolution fusion | flops 452988288 | bytes 9437472 | tf_op jit(solution)/shard_map/se,ezr->szr/dot_general | solution.py:105
  215.2 6.3 copy.99
  221.5 5.2 all-to-all-start.2
  226.8 143.3 %all-to-all-done.2 = f32[16,3,128,256]{3,2,1,0:T(8,128)} async-done(((f32[16,3,128,256]{3,2,1,0:T(8,128)}), f32[16,3,128,256]{3,2,1,0:T(8,128)}, u32[]{:S(2)}, u32[]{:S(2)}) %all-to-all-start.2) | async-done | bytes 6291488 | tf_op jit(solution)/shard_map/all_to_all | solution.py:112
  370.1 8.4 %fusion.133 = (bf16[4,128,256]{2,0,1:T(4,128)(2,1)S(1)}, f32[4,128,256]{2,0,1:T(4,128)S(1)}) fusion(f32[4]{0:T(128)S(1)} %broadcast_maximum_fusion, f32[48,128,256]{2,1,0:T(8,128)} %bitcast.22, s32[48]{0:T(128)S(1)} %eq.74, pred[4]{0:T(512)(128)(4,1)S(1)} %broadcast_compare_fusion, f32[4,128,256]{2,1,0:T(8,128)S(1)} %copy-done), kind=kOutput, calls=%fused_computation.130 | convolution fusion | flops 76021952 | bytes 7602388 | tf_op jit(solution)/shard_map/bs,szr->bzr/dot_general | solution.py:120
  378.5 1.3 collective-permute-start.4
  379.8 3.0 collective-permute-start.5
  382.9 0.8 collective-permute-done.5
  383.7 1.2 convolution_convert_fusion
  384.9 1.4 copy.102
  386.3 93.0 %all_to_all.27 = bf16[16,3,160,256]{3,2,1,0:T(8,128)(2,1)S(1)} all-to-all(bf16[16,3,160,256]{3,2,1,0:T(8,128)(2,1)S(1)} %bitcast.81), channel_id=1, replica_groups=mesh['join'=16,'view'=2] {'join'}, dimensions={0} | all-to-all | bytes 7864320 | tf_op jit(solution)/shard_map/all_to_all | solution.py:86
  479.4 2.3 fusion.41
  481.6 0.5 copy.104
  482.1 1.0 copy-done.3
  483.1 0.7 fusion.9
  483.8 1.3 collective-permute-start.6
  485.1 3.8 collective-permute-start.7
  488.9 0.9 collective-permute-done.7
  489.8 0.6 fusion.32
  490.4 0.3 copy.106
  490.7 7.3 %fusion.10 = f32[16,3,128,256]{3,0,2,1:T(8,128)S(1)} fusion(f32[24,128,256]{2,1,0:T(8,128)S(1)} %bitcast.83, s32[16,3]{0,1:T(4,128)S(1)} %multiply_add_fusion, s32[24]{0:T(128)S(1)} %add_add_fusion), kind=kOutput, calls=%fused_computation.14 | convolution fusion | flops 452988288 | bytes 9437472 | tf_op jit(solution)/shard_map/se,ezr->szr/dot_general | solution.py:105
  498.0 3.6 copy.108
  501.6 141.6 %all_to_all.28 = f32[16,3,128,256]{3,2,1,0:T(8,128)S(1)} all-to-all(f32[16,3,128,256]{3,2,1,0:T(8,128)S(1)} %copy.108), channel_id=1, replica_groups=mesh['join'=16,'view'=2] {'join'}, dimensions={0} | all-to-all | bytes 12582912 | tf_op jit(solution)/shard_map/all_to_all | solution.py:112
  643.3 5.7 fusion.57
  649.0 0.9 copy.110
  (37 shorter events, 1.8 us)
Async XLA Ops:
  1.4 18.2 %collective-permute-start = (bf16[4,16,256]{2,0,1:T(4,128)(2,1)S(1)}, bf16[4,16,256]{2,0,1:T(4,128)(2,1)S(1)}, u32[]{:S(2)}, u32[]{:S(2)}) collective-permute-start(bf16[4,16,256]{2,0,1:T(4,128)(2,1)S(1)} %get-tuple-element.12), channel_id=1, source_target_pairs={{0,1},{2,3},{4,5},{6,7},{8,9},{10,11},{12,13},{14,15},{16,17},{18,... | collective-permute-start | bytes 98312 | tf_op jit(solution)/shard_map/ppermute | solution.py:16
  2.7 16.9 %collective-permute-start.1 = (bf16[4,16,256]{2,0,1:T(4,128)(2,1)S(1)}, bf16[4,16,256]{2,0,1:T(4,128)(2,1)S(1)}, u32[]{:S(2)}, u32[]{:S(2)}) collective-permute-start(bf16[4,16,256]{2,0,1:T(4,128)(2,1)S(1)} %get-tuple-element.13), channel_id=1, source_target_pairs={{1,0},{3,2},{5,4},{7,6},{9,8},{11,10},{13,12},{15,14},{17,16},{19,... | collective-permute-start | bytes 98312 | tf_op jit(solution)/shard_map/ppermute | solution.py:19
  24.2 6.5 copy-start.1
  24.2 94.8 %all-to-all-start.1 = ((bf16[16,3,160,256]{3,2,1,0:T(8,128)(2,1)}), bf16[16,3,160,256]{3,2,1,0:T(8,128)(2,1)}, u32[]{:S(2)}, u32[]{:S(2)}) async-start(bf16[16,3,160,256]{3,2,1,0:T(8,128)(2,1)} %bitcast.80), calls=%async_computation.1 | async-start | bytes 7864320 | tf_op jit(solution)/shard_map/all_to_all | solution.py:86
  123.4 1.4 copy-start.2
  125.5 81.5 %collective-permute-start.2 = (bf16[4,6,16,256]{3,2,0,1:T(8,128)(2,1)S(1)}, bf16[4,6,16,256]{3,2,0,1:T(8,128)(2,1)S(1)}, u32[]{:S(2)}, u32[]{:S(2)}) collective-permute-start(bf16[4,6,16,256]{3,2,0,1:T(8,128)(2,1)S(1)} %get-tuple-element.8), channel_id=1, source_target_pairs={{0,1},{2,3},{4,5},{6,7},{8,9},{10,11},{12,13},{14,15},{16,17},{18,... | collective-permute-start | bytes 589832 | tf_op jit(solution)/shard_map/ppermute | solution.py:16
  126.8 80.2 %collective-permute-start.3 = (bf16[4,6,16,256]{3,2,0,1:T(8,128)(2,1)S(1)}, bf16[4,6,16,256]{3,2,0,1:T(8,128)(2,1)S(1)}, u32[]{:S(2)}, u32[]{:S(2)}) collective-permute-start(bf16[4,6,16,256]{3,2,0,1:T(8,128)(2,1)S(1)} %get-tuple-element.9), channel_id=1, source_target_pairs={{1,0},{3,2},{5,4},{7,6},{9,8},{11,10},{13,12},{15,14},{17,16},{19,... | collective-permute-start | bytes 589832 | tf_op jit(solution)/shard_map/ppermute | solution.py:19
  221.5 148.6 %copy-start = (f32[4,128,256]{2,1,0:T(8,128)S(1)}, f32[4,128,256]{2,1,0:T(8,128)}, u32[]{:S(2)}) copy-start(f32[4,128,256]{2,1,0:T(8,128)} %param.7) | copy-start | bytes 1572868
  221.5 148.6 %all-to-all-start.2 = ((f32[16,3,128,256]{3,2,1,0:T(8,128)}), f32[16,3,128,256]{3,2,1,0:T(8,128)}, u32[]{:S(2)}, u32[]{:S(2)}) async-start(f32[16,3,128,256]{3,2,1,0:T(8,128)} %copy.99), calls=%async_computation.2 | async-start | bytes 12582912 | tf_op jit(solution)/shard_map/all_to_all | solution.py:112
  378.5 4.3 collective-permute-start.4
  379.8 3.9 collective-permute-start.5
  481.6 1.4 copy-start.3
  483.8 5.1 collective-permute-start.6
  485.1 4.7 collective-permute-start.7
where the time goes:
time: 660 us; the launch traced here: 650 us
  blocking collectives  245 us (37%)
  local copies, waits for them, and re-layouts  175 us (27%)
  waiting for transfers between devices  156 us (24%)
  matrix products  40.4 us (6%)
  starting transfers between devices  30.3 us (5%)
    gather x4, local copies, waits for them, and re-layouts, toeplitz(): picked = jnp.take(kernel, jnp.clip(offset, 0, taps - 1), axis=1)  153 us
    all_to_all x1, waiting for transfers between devices, local(): lax.all_to_all(outgoing.reshape(peer_count, slot_cap, depth, lat_rows), '...  143 us
    all_to_all x1, blocking collectives, local(): lax.all_to_all(outgoing.reshape(peer_count, slot_cap, depth, lat_rows), '...  142 us
    all_to_all x1, blocking collectives, local(): lax.all_to_all(reply_buf.reshape(peer_count, slot_cap, extent, lat_rows),...  93 us
    dot_general x2, matrix products, local(): jnp.einsum('se,ezr->szr', send_full, corr_rows, precision=lax.Precision.H...  14.5 us
    dot_general x2, matrix products, local(): jnp.einsum('bs,szr->bzr', owner_onehot, returned, precision=lax.Precision...  14.1 us
    ppermute x4, starting transfers between devices, padded(): lax.ppermute(lax.slice_in_dim(block, 0, width, axis=dim), axis, backward)  13.4 us
  transfers between devices with their start and end apart: 10, of which 4 were waited for; matrix products, arithmetic and copies ran while one was open for 24% of the time, Pallas kernels for 0%

commit v1 on v0

v1 whole, which is shorter than its diff:
```python
import functools

import jax
import jax.numpy as jnp
from jax import lax
from jax.experimental import pallas as pl
from jax.experimental.pallas import tpu as pltpu
from jax.sharding import PartitionSpec as P

H = 16
CAP = 3
ITERS = 2
GROUP = 4
EST_HALO = 2 * ITERS * H
VIEW_HALO = EST_HALO - H

SMEM = pl.BlockSpec(memory_space=pltpu.SMEM)
VMEM = pl.BlockSpec(memory_space=pltpu.VMEM)
ANY = pl.BlockSpec(memory_space=pl.ANY)


def pack_kernel(cap, owners, blocks_of, views, out, table, seen, sems):
    blocks, nviews = views.shape[0], views.shape[1]
    peers = out.shape[0] // cap

    @pl.loop(0, peers)
    def _(peer):
        seen[peer] = 0

    @pl.loop(0, peers * cap)
    def _(slot):
        table[slot] = -1

    copies = []
    for i in range(blocks):
        for v in range(nviews):
            owner = owners[i, v]
            order = seen[owner]
            seen[owner] = order + 1
            slot = owner * cap + order
            table[slot] = blocks_of[i, v] * nviews + v
            copy = pltpu.make_async_copy(views.at[i, v], out.at[slot], sems.at[i * nviews + v])
            copy.start()
            copies.append(copy)
    for copy in copies:
        copy.wait()


def pack(views, owners, blocks_of, peers):
    blocks, nviews, depth, lat = views.shape
    return pl.pallas_call(
        functools.partial(pack_kernel, CAP),
        out_shape=(
            jax.ShapeDtypeStruct((peers * CAP, depth, lat), views.dtype),
            jax.ShapeDtypeStruct((peers * CAP,), jnp.int32),
        ),
        in_specs=[SMEM, SMEM, ANY],
        out_specs=(ANY, SMEM),
        scratch_shapes=[
            pltpu.SMEM((peers,), jnp.int32),
            pltpu.SemaphoreType.DMA((blocks * nviews,)),
        ],
        name="pack",
    )(owners, blocks_of, views)


def toeplitz_kernel(taps, kernel, forward, mirror):
    nviews, frame = forward.shape[0], forward.shape[1]
    row = lax.broadcasted_iota(jnp.int32, (frame, frame), 0)
    column = lax.broadcasted_iota(jnp.int32, (frame, frame), 1)
    for ref, tap_at in ((forward, column - row + H), (mirror, row - column + H)):

        @pl.loop(0, nviews)
        def _(v):
            def put(t, total):
                return jnp.where(tap_at == t, kernel[v, t], total)

            total = lax.fori_loop(0, taps, put, jnp.zeros((frame, frame), jnp.float32))
            ref[v] = total.astype(ref.dtype)


def toeplitz(kernel, frame):
    nviews, taps = kernel.shape
    shape = jax.ShapeDtypeStruct((nviews, frame, frame), jnp.bfloat16)
    return pl.pallas_call(
        functools.partial(toeplitz_kernel, taps),
        out_shape=(shape, shape),
        in_specs=[SMEM],
        out_specs=(VMEM, VMEM),
        name="toeplitz",
    )(kernel.astype(jnp.float32))


def deconvolve_kernel(
    pieces, guard, codes, offsets, *refs
):
    sources = refs[: len(pieces)]
    est, forward, mirror, out = refs[len(pieces) : len(pieces) + 4]
    held, recip, current, total, slot_of, code_of, counts, starts, sems = refs[len(pieces) + 4 :]
    nviews, frame = forward.shape[0], forward.shape[1]
    blocks, depth, lat = out.shape
    slots = codes.shape[0]
    blank = held.shape[0] - 1

    for b in range(blocks):
        counts[b] = 0

    @pl.loop(0, slots)
    def _(slot):
        code = codes[slot]

        @pl.when(code >= 0)
        def _():
            b = code // nviews
            counts[b] = counts[b] + 1
            for which, (source, rows) in enumerate(zip(sources, pieces)):
                at = pl.multiple_of(offsets[which], H)
                pltpu.make_async_copy(
                    source.at[slot], held.at[slot, pl.ds(at, rows)], sems.at[slot, which]
                ).start()

    start = jnp.int32(0)
    for b in range(blocks):
        starts[b] = start
        start = start + (counts[b] + (GROUP - 1)) // GROUP * GROUP
    starts[blocks] = start

    @pl.loop(0, slot_of.shape[0])
    def _(p):
        slot_of[p] = blank
        code_of[p] = 0

    @pl.loop(0, slots)
    def _(slot):
        code = codes[slot]

        @pl.when(code >= 0)
        def _():
            b = code // nviews
            p = starts[b]
            starts[b] = p + 1
            slot_of[p] = slot
            code_of[p] = code - b * nviews

    start = jnp.int32(0)
    for b in range(blocks):
        starts[b] = start
        start = start + (counts[b] + (GROUP - 1)) // GROUP * GROUP

    held[blank] = jnp.zeros(held.shape[1:], held.dtype)
    covered = sum(pieces)
    if covered < frame:
        edge = frame - covered
        sides = 1 if len(pieces) == 2 else 2
        for side in range(sides):
            at = pl.multiple_of(offsets[len(pieces) + side], H)

            @pl.loop(0, slots)
            def _(slot):
                held[slot, pl.ds(at, edge // sides)] = jnp.zeros((edge // sides, lat), held.dtype)

    current[...] = est[...]
    for sweep in range(ITERS):
        for b in range(blocks):

            @pl.when(counts[b] > 0)
            def _():
                rounded = current[b].astype(jnp.bfloat16)

                @pl.loop(0, nviews)
                def _(v):
                    blurred = jnp.dot(forward[v], rounded, preferred_element_type=jnp.float32)
                    inverse = 1.0 / blurred
                    if guard:
                        inverse = jnp.where(blurred > 0, inverse, 0.0)
                    recip[b, v] = inverse

        if sweep == 0:

            @pl.loop(0, slots)
            def _(slot):
                @pl.when(codes[slot] >= 0)
                def _():
                    for which, (source, rows) in enumerate(zip(sources, pieces)):
                        at = pl.multiple_of(offsets[which], H)
                        pltpu.make_async_copy(
                            source.at[slot], held.at[slot, pl.ds(at, rows)], sems.at[slot, which]
                        ).wait()

        for b in range(blocks):

            @pl.when(counts[b] > 0)
            def _():
                total[...] = jnp.zeros_like(total)

                @pl.loop(0, (counts[b] + (GROUP - 1)) // GROUP)
                def _(group):
                    first = starts[b] + group * GROUP
                    gained = None
                    for member in range(GROUP):
                        v = code_of[first + member]
                        quotient = (
                            held[slot_of[first + member]].astype(jnp.float32) * recip[b, v]
                        ).astype(jnp.bfloat16)
                        part = jnp.dot(mirror[v], quotient, preferred_element_type=jnp.float32)
                        gained = part if gained is None else gained + part
                    total[...] += gained

                current[b] = current[b] * (total[...] / counts[b].astype(jnp.float32))

    own = pl.multiple_of(offsets[0], H)
    out[...] = current[:, pl.ds(own, depth)]


def deconvolve(codes, offsets, sources, est, forward, mirror, depth, guard):
    blocks, frame, lat = est.shape
    nviews = forward.shape[0]
    slots = codes.shape[0]
    pieces = tuple(source.shape[1] for source in sources)
    listed = slots + blocks * GROUP
    return pl.pallas_call(
        functools.partial(deconvolve_kernel, pieces, guard),
        out_shape=jax.ShapeDtypeStruct((blocks, depth, lat), jnp.float32),
        in_specs=[SMEM, SMEM] + [ANY] * len(sources) + [VMEM, VMEM, VMEM],
        out_specs=VMEM,
        scratch_shapes=[
            pltpu.VMEM((slots + 1, frame, lat), jnp.bfloat16),
            pltpu.VMEM((blocks, nviews, frame, lat), jnp.float32),
            pltpu.VMEM((blocks, frame, lat), jnp.float32),
            pltpu.VMEM((frame, lat), jnp.float32),
            pltpu.SMEM((listed,), jnp.int32),
            pltpu.SMEM((listed,), jnp.int32),
            pltpu.SMEM((blocks,), jnp.int32),
            pltpu.SMEM((blocks + 1,), jnp.int32),
            pltpu.SemaphoreType.DMA((slots, len(sources))),
        ],
        compiler_params=pltpu.CompilerParams(vmem_limit_bytes=40 * 1024 * 1024),
        name="deconvolve",
    )(codes, offsets, *sources, est, forward, mirror)


def halos(block, dim, width):
    count = lax.axis_size("view")
    depth = block.shape[dim]
    if count == 1:
        return ()
    if count == 2:
        start = jnp.where(lax.axis_index("view") == 0, depth - width, 0)
        sent = lax.dynamic_slice_in_dim(block, start, width, axis=dim)
        return (lax.ppermute(sent, "view", [(0, 1), (1, 0)]),)
    forward = [(i, i + 1) for i in range(count - 1)]
    backward = [(target, source) for source, target in forward]
    low = lax.ppermute(lax.slice_in_dim(block, depth - width, depth, axis=dim), "view", forward)
    high = lax.ppermute(lax.slice_in_dim(block, 0, width, axis=dim), "view", backward)
    return (low, high)


def framed(block, sides, dim):
    if not sides:
        return block
    if len(sides) == 2:
        return jnp.concatenate([sides[0], block, sides[1]], axis=dim)
    (side,) = sides
    return jnp.where(
        lax.axis_index("view") == 0,
        jnp.concatenate([block, side], axis=dim),
        jnp.concatenate([side, block], axis=dim),
    )


def frame_offsets(depth):
    count = lax.axis_size("view")
    empty = EST_HALO - VIEW_HALO
    if count == 1:
        return jnp.zeros((1,), jnp.int32)
    if count == 2:
        first = jnp.array([0, depth, depth + VIEW_HALO], jnp.int32)
        second = jnp.array([EST_HALO, empty, 0], jnp.int32)
        return jnp.where(lax.axis_index("view") == 0, first, second)
    return jnp.array(
        [EST_HALO, empty, EST_HALO + depth, 0, EST_HALO + depth + VIEW_HALO], jnp.int32
    )


def gathered_tables(table, axis):
    count = lax.axis_size(axis)
    if count & (count - 1):
        return lax.all_gather(table, axis, axis=0)
    rows = table[None]
    here = lax.axis_index(axis)
    step = 1
    while step < count:
        other = lax.ppermute(rows, axis, [(i, i ^ step) for i in range(count)])
        rows = jnp.where(
            (here & step) == 0,
            jnp.concatenate([rows, other], axis=0),
            jnp.concatenate([other, rows], axis=0),
        )
        step *= 2
    return rows


def local(estimate, views, owners, local_blocks, psf):
    blocks, depth, lat = estimate.shape
    peers = lax.axis_size("join")
    normed = psf / jnp.sum(psf, axis=1, keepdims=True)
    kernel = normed.astype(jnp.bfloat16)

    packed, table = pack(views, owners, local_blocks, peers)
    arrived = lax.all_to_all(
        packed.reshape(peers, CAP, depth, lat), "join", split_axis=0, concat_axis=0, tiled=True
    ).reshape(peers * CAP, depth, lat)

    tables = gathered_tables(table, "join").reshape(peers, peers, CAP)
    codes = lax.dynamic_index_in_dim(tables, lax.axis_index("join"), axis=1, keepdims=False)
    est = framed(estimate, halos(estimate, 1, EST_HALO), 1)
    forward, mirror = toeplitz(kernel, est.shape[1])

    sides = halos(arrived, 1, VIEW_HALO)
    return deconvolve(
        codes.reshape(-1),
        frame_offsets(depth),
        (arrived,) + sides,
        est,
        forward,
        mirror,
        depth,
        lax.axis_size("view") > 2,
    )


def solution(mesh):
    in_specs = (
        P("join", "view", None),
        P("join", None, "view", None),
        P("join", None),
        P("join", None),
        P(),
    )
    out_specs = P("join", "view", None)
    return jax.shard_map(local, mesh=mesh, in_specs=in_specs, out_specs=out_specs, check_vma=False)
```

time: 660 us -> 187 us (0.28)
  the two profiles are of different devices: /device:TPU:13 before, /device:TPU:14 now
where the time goes in v1:
time: 187 us; the launch traced here: 188 us
  Pallas kernels  93.5 us (50%)
  waiting for transfers between devices  78.4 us (42%)
  starting transfers between devices  8.61 us (5%)
  local copies, waits for them, and re-layouts  3.88 us (2%)
  other arithmetic  3.19 us (2%)
    all_to_all x1, waiting for transfers between devices, local(): lax.all_to_all(packed.reshape(peers, CAP, depth, lat), 'join', split_axis...  69.1 us
    pallas_call x1, Pallas kernels, pack(): pl.pallas_call(functools.partial(pack_kernel, CAP), out_shape=(jax.ShapeD...  50.6 us
    pallas_call x1, Pallas kernels, deconvolve(): pl.pallas_call(functools.partial(deconvolve_kernel, pieces, guard), out_s...  24.2 us
    pallas_call x1, Pallas kernels, toeplitz(): pl.pallas_call(functools.partial(toeplitz_kernel, taps), out_shape=(shape...  18.8 us
    ppermute x4, waiting for transfers between devices, gathered_tables(): other = lax.ppermute(rows, axis, [(i, i ^ step) for i in range(count)])  9.31 us
    all_to_all x1, starting transfers between devices, local(): lax.all_to_all(packed.reshape(peers, CAP, depth, lat), 'join', split_axis...  7.15 us
  transfers between devices with their start and end apart: 7, of which 4 were waited for; matrix products, arithmetic and copies ran while one was open for 4% of the time, Pallas kernels for 10%

profile of v1, /device:TPU:14, one launch (start us, length us, event | category | flops | bytes accessed | tf_op | source)
XLA Modules:
  0.0 187.8 jit_solution(10187415940559601323)
XLA Ops:
  0.0 50.6 %pack.1 = (bf16[48,128,256]{2,1,0:T(8,128)(2,1)}, s32[48]{0:T(128)}) custom-call(s32[4,6]{1,0:T(4,128)} %owners.1, s32[4,6]{1,0:T(4,128)} %blocks_of.1, bf16[4,6,128,256]{3,2,1,0:T(8,128)(2,1)} %views.1), custom_call_target="tpu_custom_call" | custom-call | tf_op jit(solution)/shard_map/pack/pallas_call | solution.py:51
  50.6 0.0 copy-start.3
  50.6 7.2 %all-to-all-start = ((bf16[16,3,128,256]{3,2,1,0:T(8,128)(2,1)}), bf16[16,3,128,256]{3,2,1,0:T(8,128)(2,1)S(1)}, u32[]{:S(2)}, u32[]{:S(2)}) async-start(bf16[16,3,128,256]{3,2,1,0:T(8,128)(2,1)} %bitcast.9), calls=%async_computation | async-start | bytes 6291456 | tf_op jit(solution)/shard_map/all_to_all | solution.py:310
  57.8 0.0 copy-start.5
  57.8 0.0 copy-start.2
  57.8 0.0 copy-done.3
  57.8 0.6 collective-permute-start
  58.4 1.0 constant_dynamic-slice_fusion
  59.4 0.1 collective-permute-start.5
  59.5 69.1 %all-to-all-done = bf16[16,3,128,256]{3,2,1,0:T(8,128)(2,1)S(1)} async-done(((bf16[16,3,128,256]{3,2,1,0:T(8,128)(2,1)}), bf16[16,3,128,256]{3,2,1,0:T(8,128)(2,1)S(1)}, u32[]{:S(2)}, u32[]{:S(2)}) %all-to-all-start) | async-done | bytes 3145760 | tf_op jit(solution)/shard_map/all_to_all | solution.py:310
  128.6 1.1 constant_dynamic-slice_fusion.1
  129.7 0.0 collective-permute-start.4
  129.7 0.0 copy-done.4
  129.7 0.0 copy-done.5
  129.7 0.1 concatenate.60
  129.8 0.1 copy.11
  129.9 0.0 copy-done.2
  129.9 0.1 reduce_sum.9
  130.0 0.7 fusion.1.kernel
  130.7 18.8 %toeplitz.1 = (bf16[6,192,192]{2,1,0:T(8,128)(2,1)}, bf16[6,192,192]{2,1,0:T(8,128)(2,1)}) custom-call(f32[6,33]{1,0:T(8,128)} %fusion.1.kernel), custom_call_target="tpu_custom_call" | custom-call | tf_op jit(solution)/shard_map/toeplitz/pallas_call | solution.py:85
  149.5 0.0 collective-permute-done
  149.5 0.1 collective-permute-start.1
  149.6 0.5 broadcast.8
  150.1 0.7 reduce.3
  150.7 0.1 concatenate.61
  150.8 0.1 copy.12
  150.9 2.2 %collective-permute-done.1 = s32[2,48]{1,0:T(2,128)S(1)} collective-permute-done((s32[2,48]{1,0:T(2,128)S(1)}, s32[2,48]{1,0:T(2,128)S(1)}, u32[]{:S(2)}, u32[]{:S(2)}) %collective-permute-start.1) | collective-permute-done | bytes 416 | tf_op jit(solution)/shard_map/ppermute | solution.py:293
  153.1 0.1 collective-permute-start.2
  153.2 0.1 concatenate.66
  153.3 0.1 copy.15
  153.4 3.4 %collective-permute-done.2 = s32[4,48]{1,0:T(4,128)S(1)} collective-permute-done((s32[4,48]{1,0:T(4,128)S(1)}, s32[4,48]{1,0:T(4,128)S(1)}, u32[]{:S(2)}, u32[]{:S(2)}) %collective-permute-start.2) | collective-permute-done | bytes 800 | tf_op jit(solution)/shard_map/ppermute | solution.py:293
  156.8 0.6 collective-permute-start.3
  157.4 0.1 concatenate.71
  157.5 0.1 copy.17
  157.6 3.7 %collective-permute-done.3 = s32[8,48]{1,0:T(8,128)S(1)} collective-permute-done((s32[8,48]{1,0:T(8,128)S(1)}, s32[8,48]{1,0:T(8,128)S(1)}, u32[]{:S(2)}, u32[]{:S(2)}) %collective-permute-start.3) | collective-permute-done | bytes 1568 | tf_op jit(solution)/shard_map/ppermute | solution.py:293
  161.4 0.1 copy.19
  161.5 0.1 copy.20
  161.5 0.1 fusion
  161.6 0.2 copy.22
  161.8 0.1 reshape.30.codes
  161.9 0.0 copy-start
  161.9 0.0 copy-start.1
  161.9 0.0 collective-permute-done.5
  161.9 1.6 maximum_select_fusion.refs_2_
  163.5 0.0 collective-permute-done.4.refs_1_
  163.5 0.0 copy-done
  163.5 0.1 copy-done.1
  163.6 24.2 %deconvolve.1 = f32[4,128,256]{2,1,0:T(8,128)} custom-call(s32[48]{0:T(128)S(1)} %reshape.30.codes, s32[3]{0:T(128)S(1)} %broadcast_select_fusion.offsets, bf16[48,128,256]{2,1,0:T(8,128)(2,1)S(1)} %bitcast.8, bf16[48,48,256]{2,1,0:T(8,128)(2,1)} %collective-permute-done.4.refs_1_, f32[4,192,256]{2,1,0:T(8,128)S(1)} %maximum_select_fusion.refs_2_, ...), custom_call_target="tpu_custom_call" | custom-call | tf_op jit(solution)/shard_map/deconvolve/pallas_call | solution.py:221
  (9 shorter events, 0.1 us)
Async XLA Ops:
  50.6 7.2 %copy-start.3 = (s32[48]{0:T(128)S(1)}, s32[48]{0:T(128)}, u32[]{:S(2)}) copy-start(s32[48]{0:T(128)} %get-tuple-element.9) | copy-start | bytes 580
  50.6 78.0 %all-to-all-start = ((bf16[16,3,128,256]{3,2,1,0:T(8,128)(2,1)}), bf16[16,3,128,256]{3,2,1,0:T(8,128)(2,1)S(1)}, u32[]{:S(2)}, u32[]{:S(2)}) async-start(bf16[16,3,128,256]{3,2,1,0:T(8,128)(2,1)} %bitcast.9), calls=%async_computation | async-start | bytes 6291456 | tf_op jit(solution)/shard_map/all_to_all | solution.py:310
  57.8 71.9 %copy-start.4 = (s32[3]{0:T(128)S(1)}, s32[3]{0:T(128)}, u32[]{:S(2)}) copy-start(s32[3]{0:T(128)} %constant.36.clone) | copy-start | bytes 40
  57.8 71.9 %copy-start.5 = (s32[3]{0:T(128)S(1)}, s32[3]{0:T(128)}, u32[]{:S(2)}) copy-start(s32[3]{0:T(128)} %constant.37.clone) | copy-start | bytes 40
  57.8 72.1 %copy-start.2 = (f32[6,33]{1,0:T(8,128)S(1)}, f32[6,33]{1,0:T(8,128)}, u32[]{:S(2)}) copy-start(f32[6,33]{1,0:T(8,128)} %param.11) | copy-start | bytes 2380
  57.8 91.6 %collective-permute-start = (s32[1,48]{1,0:T(1,128)S(1)}, s32[1,48]{1,0:T(1,128)S(1)}, u32[]{:S(2)}, u32[]{:S(2)}) collective-permute-start(s32[1,48]{1,0:T(1,128)S(1)} %bitcast.10), channel_id=1, source_target_pairs={{0,2},{2,0},{4,6},{6,4},{8,10},{10,8},{12,14},{14,12},{16,18},{18,... | collective-permute-start | bytes 584 | tf_op jit(solution)/shard_map/ppermute | solution.py:293
  59.4 102.5 %collective-permute-start.5 = (f32[4,64,256]{2,1,0:T(8,128)S(1)}, f32[4,64,256]{2,1,0:T(8,128)}, u32[]{:S(2)}, u32[]{:S(2)}) collective-permute-start(f32[4,64,256]{2,1,0:T(8,128)S(1)} %constant_dynamic-slice_fusion), channel_id=1, source_target_pairs={{0,1},{1,0},{2,3},{3,2},{4,5},{5,4},{6,7},{7,6},{8,9},{9,8},{10,11... | collective-permute-start | bytes 786440 | tf_op jit(solution)/shard_map/ppermute | solution.py:250
  129.7 33.8 %collective-permute-start.4 = (bf16[48,48,256]{2,1,0:T(8,128)(2,1)}, bf16[48,48,256]{2,1,0:T(8,128)(2,1)}, u32[]{:S(2)}, u32[]{:S(2)}) collective-permute-start(bf16[48,48,256]{2,1,0:T(8,128)(2,1)} %constant_dynamic-slice_fusion.1), channel_id=1, source_target_pairs={{0,1},{1,0},{2,3},{3,2},{4,5},{5,4},{6,7},{7,6},{8,9},{9,8},{10,11... | collective-permute-start | bytes 3538952 | tf_op jit(solution)/shard_map/ppermute | solution.py:250
  149.5 3.6 %collective-permute-start.1 = (s32[2,48]{1,0:T(2,128)S(1)}, s32[2,48]{1,0:T(2,128)S(1)}, u32[]{:S(2)}, u32[]{:S(2)}) collective-permute-start(s32[2,48]{1,0:T(2,128)S(1)} %add_select_fusion.5), channel_id=1, source_target_pairs={{0,4},{2,6},{4,0},{6,2},{8,12},{10,14},{12,8},{14,10},{16,20},{18,... | collective-permute-start | bytes 1160 | tf_op jit(solution)/shard_map/ppermute | solution.py:293
  153.1 3.7 %collective-permute-start.2 = (s32[4,48]{1,0:T(4,128)S(1)}, s32[4,48]{1,0:T(4,128)S(1)}, u32[]{:S(2)}, u32[]{:S(2)}) collective-permute-start(s32[4,48]{1,0:T(4,128)S(1)} %add_select_fusion.4), channel_id=1, source_target_pairs={{0,8},{2,10},{4,12},{6,14},{8,0},{10,2},{12,4},{14,6},{16,24},{18,... | collective-permute-start | bytes 2312 | tf_op jit(solution)/shard_map/ppermute | solution.py:293
  156.8 4.6 %collective-permute-start.3 = (s32[8,48]{1,0:T(8,128)S(1)}, s32[8,48]{1,0:T(8,128)S(1)}, u32[]{:S(2)}, u32[]{:S(2)}) collective-permute-start(s32[8,48]{1,0:T(8,128)S(1)} %add_select_fusion.2), channel_id=1, source_target_pairs={{0,16},{2,18},{4,20},{6,22},{8,24},{10,26},{12,28},{14,30},{16,0},... | collective-permute-start | bytes 4616 | tf_op jit(solution)/shard_map/ppermute | solution.py:293
  161.9 1.6 copy-start
  161.9 1.7 copy-start.1

commit v2 on v1

--- a/solution.py
+++ b/solution.py
@@ -19,9 +19,16 @@
 ANY = pl.BlockSpec(memory_space=pl.ANY)
 
 
-def pack_kernel(cap, owners, blocks_of, views, out, table, seen, sems):
+def pack_kernel(cap, owners, blocks_of, views, out, table, seen, staged, in_sems, out_sems):
     blocks, nviews = views.shape[0], views.shape[1]
     peers = out.shape[0] // cap
+
+    pairs = [(i, v) for i in range(blocks) for v in range(nviews)]
+    loads = [
+        pltpu.make_async_copy(views.at[i, v], staged.at[i, v], in_sems.at[i, v]) for i, v in pairs
+    ]
+    for load in loads:
+        load.start()
 
     @pl.loop(0, peers)
     def _(peer):
@@ -31,19 +38,19 @@
     def _(slot):
         table[slot] = -1
 
-    copies = []
-    for i in range(blocks):
-        for v in range(nviews):
-            owner = owners[i, v]
-            order = seen[owner]
-            seen[owner] = order + 1
-            slot = owner * cap + order
-            table[slot] = blocks_of[i, v] * nviews + v
-            copy = pltpu.make_async_copy(views.at[i, v], out.at[slot], sems.at[i * nviews + v])
-            copy.start()
-            copies.append(copy)
-    for copy in copies:
-        copy.wait()
+    stores = []
+    for (i, v), load in zip(pairs, loads):
+        owner = owners[i, v]
+        order = seen[owner]
+        seen[owner] = order + 1
+        slot = owner * cap + order
+        table[slot] = blocks_of[i, v] * nviews + v
+        load.wait()
+        store = pltpu.make_async_copy(staged.at[i, v], out.at[slot], out_sems.at[i, v])
+        store.start()
+        stores.append(store)
+    for store in stores:
+        store.wait()
 
 
 def pack(views, owners, blocks_of, peers):
@@ -58,7 +65,9 @@
         out_specs=(ANY, SMEM),
         scratch_shapes=[
             pltpu.SMEM((peers,), jnp.int32),
-            pltpu.SemaphoreType.DMA((blocks * nviews,)),
+            pltpu.VMEM(views.shape, views.dtype),
+            pltpu.SemaphoreType.DMA((blocks, nviews)),
+            pltpu.SemaphoreType.DMA((blocks, nviews)),
         ],
         name="pack",
     )(owners, blocks_of, views)
@@ -315,6 +324,9 @@
     codes = lax.dynamic_index_in_dim(tables, lax.axis_index("join"), axis=1, keepdims=False)
     est = framed(estimate, halos(estimate, 1, EST_HALO), 1)
     forward, mirror = toeplitz(kernel, est.shape[1])
+    arrived, codes, est, forward, mirror = lax.optimization_barrier(
+        (arrived, codes, est, forward, mirror)
+    )
 
     sides = halos(arrived, 1, VIEW_HALO)
     return deconvolve(

time: 187 us -> 115 us (0.61)
  the two profiles are of different devices: /device:TPU:14 before, /device:TPU:25 now
where the time goes in v2:
time: 115 us
  Pallas kernels  46.7 us (41%)
  waiting for transfers between devices  41.8 us (36%)
  starting transfers between devices  15.2 us (13%)
  local copies, waits for them, and re-layouts  6.91 us (6%)
  other arithmetic  4.22 us (4%)
    ppermute x4, waiting for transfers between devices, gathered_tables(): other = lax.ppermute(rows, axis, [(i, i ^ step) for i in range(count)])  39.1 us
    pallas_call x1, Pallas kernels, deconvolve(): pl.pallas_call(functools.partial(deconvolve_kernel, pieces, guard), out_s...  24.2 us
    pallas_call x1, Pallas kernels, toeplitz(): pl.pallas_call(functools.partial(toeplitz_kernel, taps), out_shape=(shape...  18.7 us
    all_to_all x1, starting transfers between devices, local(): lax.all_to_all(packed.reshape(peers, CAP, depth, lat), 'join', split_axis...  6.45 us
    ppermute x4, starting transfers between devices, gathered_tables(): other = lax.ppermute(rows, axis, [(i, i ^ step) for i in range(count)])  5.02 us
    pallas_call x1, Pallas kernels, pack(): pl.pallas_call(functools.partial(pack_kernel, CAP), out_shape=(jax.ShapeD...  3.79 us
    ppermute x2, starting transfers between devices, halos(): return (lax.ppermute(sent, 'view', [(0, 1), (1, 0)]),)  3.74 us
    unnamed x14, local copies, waits for them, and re-layouts  3.28 us
  transfers between devices with their start and end apart: 7, of which 4 were waited for; matrix products, arithmetic and copies ran while one was open for 6% of the time, Pallas kernels for 16%

profile of v2, /device:TPU:25, one launch (start us, length us, event | category | flops | bytes accessed | tf_op | source)
XLA Modules:
  0.0 114.9 jit_solution(17159761133941543020)
XLA Ops:
  0.0 3.8 %pack.1 = (bf16[48,128,256]{2,1,0:T(8,128)(2,1)}, s32[48]{0:T(128)}) custom-call(s32[4,6]{1,0:T(4,128)} %owners.1, s32[4,6]{1,0:T(4,128)} %blocks_of.1, bf16[4,6,128,256]{3,2,1,0:T(8,128)(2,1)} %views.1), custom_call_target="tpu_custom_call" | custom-call | tf_op jit(solution)/shard_map/pack/pallas_call | solution.py:58
  3.8 0.0 copy-start.4
  3.8 0.0 copy-start.3
  3.8 6.4 %all-to-all-start = ((bf16[16,3,128,256]{3,2,1,0:T(8,128)(2,1)}), bf16[16,3,128,256]{3,2,1,0:T(8,128)(2,1)S(1)}, u32[]{:S(2)}, u32[]{:S(2)}) async-start(bf16[16,3,128,256]{3,2,1,0:T(8,128)(2,1)} %bitcast.7), calls=%async_computation | async-start | bytes 6291456 | tf_op jit(solution)/shard_map/all_to_all | solution.py:319
  10.3 0.0 copy-done.4
  10.3 1.2 %collective-permute-start = (s32[1,48]{1,0:T(1,128)S(1)}, s32[1,48]{1,0:T(1,128)S(1)}, u32[]{:S(2)}, u32[]{:S(2)}) collective-permute-start(s32[1,48]{1,0:T(1,128)S(1)} %bitcast.8), channel_id=1, source_target_pairs={{0,2},{2,0},{4,6},{6,4},{8,10},{10,8},{12,14},{14,12},{16,18},{18,... | collective-permute-start | bytes 584 | tf_op jit(solution)/shard_map/ppermute | solution.py:302
  11.5 1.0 constant_dynamic-slice_fusion.1
  12.5 1.6 %collective-permute-start.4 = (f32[4,64,256]{2,1,0:T(8,128)S(1)}, f32[4,64,256]{2,1,0:T(8,128)}, u32[]{:S(2)}, u32[]{:S(2)}) collective-permute-start(f32[4,64,256]{2,1,0:T(8,128)S(1)} %constant_dynamic-slice_fusion.1), channel_id=1, source_target_pairs={{0,1},{1,0},{2,3},{3,2},{4,5},{5,4},{6,7},{7,6},{8,9},{9,8},{10,11... | collective-permute-start | bytes 786440 | tf_op jit(solution)/shard_map/ppermute | solution.py:259
  14.1 0.1 concatenate.60
  14.2 0.1 copy.27
  14.2 0.0 copy-done.3
  14.2 0.1 reduce_sum.9
  14.4 0.7 fusion.2.kernel
  15.0 18.7 %toeplitz.1 = (bf16[6,192,192]{2,1,0:T(8,128)(2,1)}, bf16[6,192,192]{2,1,0:T(8,128)(2,1)}) custom-call(f32[6,33]{1,0:T(8,128)} %fusion.2.kernel), custom_call_target="tpu_custom_call" | custom-call | tf_op jit(solution)/shard_map/toeplitz/pallas_call | solution.py:94
  33.8 0.0 collective-permute-done
  33.8 1.2 %collective-permute-start.1 = (s32[2,48]{1,0:T(2,128)S(1)}, s32[2,48]{1,0:T(2,128)S(1)}, u32[]{:S(2)}, u32[]{:S(2)}) collective-permute-start(s32[2,48]{1,0:T(2,128)S(1)} %add_select_fusion.5), channel_id=1, source_target_pairs={{0,4},{2,6},{4,0},{6,2},{8,12},{10,14},{12,8},{14,10},{16,20},{18,... | collective-permute-start | bytes 1160 | tf_op jit(solution)/shard_map/ppermute | solution.py:302
  35.1 0.5 broadcast.9
  35.6 0.7 reduce.5
  36.2 0.1 concatenate.61
  36.3 0.1 copy.28
  36.4 0.3 collective-permute-done.1
  36.7 0.1 collective-permute-start.2
  36.8 0.1 concatenate.66
  36.9 0.1 copy.31
  37.0 23.4 %collective-permute-done.2 = s32[4,48]{1,0:T(4,128)S(1)} collective-permute-done((s32[4,48]{1,0:T(4,128)S(1)}, s32[4,48]{1,0:T(4,128)S(1)}, u32[]{:S(2)}, u32[]{:S(2)}) %collective-permute-start.2) | collective-permute-done | bytes 800 | tf_op jit(solution)/shard_map/ppermute | solution.py:302
  60.4 2.4 %collective-permute-start.3 = (s32[8,48]{1,0:T(8,128)S(1)}, s32[8,48]{1,0:T(8,128)S(1)}, u32[]{:S(2)}, u32[]{:S(2)}) collective-permute-start(s32[8,48]{1,0:T(8,128)S(1)} %add_select_fusion.2), channel_id=1, source_target_pairs={{0,16},{2,18},{4,20},{6,22},{8,24},{10,26},{12,28},{14,30},{16,0},... | collective-permute-start | bytes 4616 | tf_op jit(solution)/shard_map/ppermute | solution.py:302
  62.9 0.1 concatenate.71
  63.0 0.1 copy.33
  63.1 15.4 %collective-permute-done.3 = s32[8,48]{1,0:T(8,128)S(1)} collective-permute-done((s32[8,48]{1,0:T(8,128)S(1)}, s32[8,48]{1,0:T(8,128)S(1)}, u32[]{:S(2)}, u32[]{:S(2)}) %collective-permute-start.3) | collective-permute-done | bytes 1568 | tf_op jit(solution)/shard_map/ppermute | solution.py:302
  78.5 0.1 copy.35
  78.6 0.1 copy.36
  78.7 0.2 fusion.1
  78.9 0.0 collective-permute-done.4
  78.9 2.4 %maximum_select_fusion.refs_2_ = f32[4,192,256]{2,1,0:T(8,128)} fusion(f32[4,64,256]{2,1,0:T(8,128)} %collective-permute-done.4, f32[4,128,256]{2,1,0:T(8,128)} %param.7, pred[]{:T(512)S(6)} %eq.22), kind=kLoop, calls=%fused_computation | loop fusion | flops 589824 | bytes 1572865 | tf_op jit(solution)/shard_map/jit(_where)/select_n | solution.py:273
  81.4 0.0 copy-start.5
  81.4 0.0 copy-start.6
  81.4 0.0 all-to-all-done
  81.4 1.1 constant_dynamic-slice_fusion
  82.5 2.2 %collective-permute-start.5 = (bf16[48,48,256]{2,1,0:T(8,128)(2,1)}, bf16[48,48,256]{2,1,0:T(8,128)(2,1)}, u32[]{:S(2)}, u32[]{:S(2)}) collective-permute-start(bf16[48,48,256]{2,1,0:T(8,128)(2,1)} %constant_dynamic-slice_fusion), channel_id=1, source_target_pairs={{0,1},{1,0},{2,3},{3,2},{4,5},{5,4},{6,7},{7,6},{8,9},{9,8},{10,11... | collective-permute-start | bytes 3538952 | tf_op jit(solution)/shard_map/ppermute | solution.py:259
  84.7 0.0 copy-done.5
  84.7 0.0 copy-done.6
  84.7 0.1 copy.38
  84.8 0.1 reshape.31.codes
  84.9 2.6 %collective-permute-done.5.refs_1_ = bf16[48,48,256]{2,1,0:T(8,128)(2,1)} collective-permute-done((bf16[48,48,256]{2,1,0:T(8,128)(2,1)}, bf16[48,48,256]{2,1,0:T(8,128)(2,1)}, u32[]{:S(2)}, u32[]{:S(2)}) %collective-permute-start.5) | collective-permute-done | bytes 1179680 | tf_op jit(solution)/shard_map/ppermute | solution.py:259
  87.5 1.1 copy-done
  88.6 1.1 copy-done.1
  89.7 1.1 copy-done.2
  90.8 24.2 %deconvolve.1 = f32[4,128,256]{2,1,0:T(8,128)} custom-call(s32[48]{0:T(128)S(1)} %reshape.31.codes, s32[3]{0:T(128)S(1)} %broadcast_select_fusion.offsets, bf16[48,128,256]{2,1,0:T(8,128)(2,1)S(1)} %bitcast.6, bf16[48,48,256]{2,1,0:T(8,128)(2,1)} %collective-permute-done.5.refs_1_, f32[4,192,256]{2,1,0:T(8,128)S(1)} %copy-done, ...), custom_call_target="tpu_custom_call" | custom-call | tf_op jit(solution)/shard_map/deconvolve/pallas_call | solution.py:230
  (11 shorter events, 0.1 us)
Async XLA Ops:
  3.8 6.5 %copy-start.4 = (s32[48]{0:T(128)S(1)}, s32[48]{0:T(128)}, u32[]{:S(2)}) copy-start(s32[48]{0:T(128)} %get-tuple-element.15) | copy-start | bytes 580
  3.8 10.4 %copy-start.3 = (f32[6,33]{1,0:T(8,128)S(1)}, f32[6,33]{1,0:T(8,128)}, u32[]{:S(2)}) copy-start(f32[6,33]{1,0:T(8,128)} %param.11) | copy-start | bytes 2380
  3.8 77.6 %all-to-all-start = ((bf16[16,3,128,256]{3,2,1,0:T(8,128)(2,1)}), bf16[16,3,128,256]{3,2,1,0:T(8,128)(2,1)S(1)}, u32[]{:S(2)}, u32[]{:S(2)}) async-start(bf16[16,3,128,256]{3,2,1,0:T(8,128)(2,1)} %bitcast.7), calls=%async_computation | async-start | bytes 6291456 | tf_op jit(solution)/shard_map/all_to_all | solution.py:319
  10.3 23.5 %collective-permute-start = (s32[1,48]{1,0:T(1,128)S(1)}, s32[1,48]{1,0:T(1,128)S(1)}, u32[]{:S(2)}, u32[]{:S(2)}) collective-permute-start(s32[1,48]{1,0:T(1,128)S(1)} %bitcast.8), channel_id=1, source_target_pairs={{0,2},{2,0},{4,6},{6,4},{8,10},{10,8},{12,14},{14,12},{16,18},{18,... | collective-permute-start | bytes 584 | tf_op jit(solution)/shard_map/ppermute | solution.py:302
  12.5 66.4 %collective-permute-start.4 = (f32[4,64,256]{2,1,0:T(8,128)S(1)}, f32[4,64,256]{2,1,0:T(8,128)}, u32[]{:S(2)}, u32[]{:S(2)}) collective-permute-start(f32[4,64,256]{2,1,0:T(8,128)S(1)} %constant_dynamic-slice_fusion.1), channel_id=1, source_target_pairs={{0,1},{1,0},{2,3},{3,2},{4,5},{5,4},{6,7},{7,6},{8,9},{9,8},{10,11... | collective-permute-start | bytes 786440 | tf_op jit(solution)/shard_map/ppermute | solution.py:259
  33.8 2.9 %collective-permute-start.1 = (s32[2,48]{1,0:T(2,128)S(1)}, s32[2,48]{1,0:T(2,128)S(1)}, u32[]{:S(2)}, u32[]{:S(2)}) collective-permute-start(s32[2,48]{1,0:T(2,128)S(1)} %add_select_fusion.5), channel_id=1, source_target_pairs={{0,4},{2,6},{4,0},{6,2},{8,12},{10,14},{12,8},{14,10},{16,20},{18,... | collective-permute-start | bytes 1160 | tf_op jit(solution)/shard_map/ppermute | solution.py:302
  36.7 23.7 %collective-permute-start.2 = (s32[4,48]{1,0:T(4,128)S(1)}, s32[4,48]{1,0:T(4,128)S(1)}, u32[]{:S(2)}, u32[]{:S(2)}) collective-permute-start(s32[4,48]{1,0:T(4,128)S(1)} %add_select_fusion.4), channel_id=1, source_target_pairs={{0,8},{2,10},{4,12},{6,14},{8,0},{10,2},{12,4},{14,6},{16,24},{18,... | collective-permute-start | bytes 2312 | tf_op jit(solution)/shard_map/ppermute | solution.py:302
  60.4 18.1 %collective-permute-start.3 = (s32[8,48]{1,0:T(8,128)S(1)}, s32[8,48]{1,0:T(8,128)S(1)}, u32[]{:S(2)}, u32[]{:S(2)}) collective-permute-start(s32[8,48]{1,0:T(8,128)S(1)} %add_select_fusion.2), channel_id=1, source_target_pairs={{0,16},{2,18},{4,20},{6,22},{8,24},{10,26},{12,28},{14,30},{16,0},... | collective-permute-start | bytes 4616 | tf_op jit(solution)/shard_map/ppermute | solution.py:302
  81.4 3.3 %copy-start.5 = (s32[3]{0:T(128)S(1)}, s32[3]{0:T(128)}, u32[]{:S(2)}) copy-start(s32[3]{0:T(128)} %constant.36.clone) | copy-start | bytes 40
  81.4 3.3 %copy-start.6 = (s32[3]{0:T(128)S(1)}, s32[3]{0:T(128)}, u32[]{:S(2)}) copy-start(s32[3]{0:T(128)} %constant.37.clone) | copy-start | bytes 40
  82.5 5.0 %collective-permute-start.5 = (bf16[48,48,256]{2,1,0:T(8,128)(2,1)}, bf16[48,48,256]{2,1,0:T(8,128)(2,1)}, u32[]{:S(2)}, u32[]{:S(2)}) collective-permute-start(bf16[48,48,256]{2,1,0:T(8,128)(2,1)} %constant_dynamic-slice_fusion), channel_id=1, source_target_pairs={{0,1},{1,0},{2,3},{3,2},{4,5},{5,4},{6,7},{7,6},{8,9},{9,8},{10,11... | collective-permute-start | bytes 3538952 | tf_op jit(solution)/shard_map/ppermute | solution.py:259
  87.5 1.1 copy-start
  88.6 1.1 copy-start.1
  89.7 1.1 copy-start.2

commit v3 on v0

v3 whole, which is shorter than its diff:
```python
import functools

import jax
import jax.numpy as jnp
from jax import lax
from jax.experimental import pallas as pl
from jax.experimental.pallas import tpu as pltpu
from jax.sharding import PartitionSpec as P

H = 16
CAP = 3
MAIN = 2
ITERS = 2
GROUP = 8
TILE = 16
EST_HALO = 2 * ITERS * H
VIEW_HALO = EST_HALO - H

SMEM = pl.BlockSpec(memory_space=pltpu.SMEM)
VMEM = pl.BlockSpec(memory_space=pltpu.VMEM)
ANY = pl.BlockSpec(memory_space=pl.ANY)


def pack_kernel(owners, blocks_of, here, views, main, *refs):
    rows, (table, seen, taken, staged, table_rows, in_sems, out_sems, table_sems) = refs[:-8], refs[-8:]
    blocks, nviews, depth, lat = views.shape
    peers, groups = seen.shape[0], len(rows)
    members = peers // groups
    pairs = [(i, v) for i in range(blocks) for v in range(nviews)]
    loads = [
        pltpu.make_async_copy(views.at[i, v], staged.at[i, v], in_sems.at[i, v]) for i, v in pairs
    ]
    for load in loads:
        load.start()

    @pl.loop(0, peers)
    def _(peer):
        seen[peer] = 0

    for group in range(groups):
        taken[group] = 0

    @pl.loop(0, peers * CAP)
    def _(slot):
        table[slot] = -1

    table[peers * CAP] = 0
    stores = []
    for (i, v), load in zip(pairs, loads):
        owner = owners[i, v]
        order = seen[owner]
        seen[owner] = order + 1
        table[owner * CAP + order] = blocks_of[i, v] * nviews + v
        away = lax.rem(owner // members + groups - here[0], groups)
        in_main = order < MAIN
        in_rows = jnp.logical_and(jnp.logical_not(in_main), taken[away] == 0)
        load.wait()

        @pl.when(in_main)
        def _():
            pltpu.make_async_copy(
                staged.at[i, v], main.at[owner * MAIN + order], out_sems.at[i, v]
            ).start()

        @pl.when(jnp.logical_not(in_main))
        def _():
            table[peers * CAP] = jnp.where(in_rows, table[peers * CAP], 1)
            for k in range(groups):

                @pl.when(jnp.logical_and(in_rows, away == k))
                def _():
                    taken[k] = 1
                    pltpu.make_async_copy(
                        staged.at[i, v], rows[k].at[0, pl.ds(0, depth)], out_sems.at[i, v]
                    ).start()

        stores.append((i, v, jnp.logical_or(in_main, in_rows)))

    lane = lax.broadcasted_iota(jnp.int32, (TILE, lat), 1)
    row = jnp.full((TILE, lat), -1, jnp.int32)
    for slot in range(peers * CAP + 1):
        row = jnp.where(lane == slot, table[slot], row)
    table_rows[...] = row.astype(jnp.float32).astype(table_rows.dtype)
    table_stores = [
        pltpu.make_async_copy(table_rows, rows[k].at[0, pl.ds(depth, TILE)], table_sems.at[k])
        for k in range(groups)
    ]
    for store in table_stores:
        store.start()
    for i, v, stored in stores:

        @pl.when(stored)
        def _():
            pltpu.make_async_copy(staged.at[i, v], main.at[0], out_sems.at[i, v]).wait()

    for store in table_stores:
        store.wait()


def pack(views, owners, blocks_of, here, peers, groups):
    blocks, nviews, depth, lat = views.shape
    assert peers * CAP < lat
    return pl.pallas_call(
        pack_kernel,
        out_shape=(jax.ShapeDtypeStruct((peers * MAIN, depth, lat), views.dtype),)
        + (jax.ShapeDtypeStruct((1, depth + TILE, lat), views.dtype),) * groups,
        in_specs=[SMEM, SMEM, SMEM, ANY],
        out_specs=(ANY,) * (1 + groups),
        scratch_shapes=[
            pltpu.SMEM((peers * CAP + 1,), jnp.int32),
            pltpu.SMEM((peers,), jnp.int32),
            pltpu.SMEM((groups,), jnp.int32),
            pltpu.VMEM(views.shape, views.dtype),
            pltpu.VMEM((TILE, lat), views.dtype),
            pltpu.SemaphoreType.DMA((blocks, nviews)),
            pltpu.SemaphoreType.DMA((blocks, nviews)),
            pltpu.SemaphoreType.DMA((groups,)),
        ],
        name="pack",
    )(owners, blocks_of, here, views)


def all_thirds_kernel(owners, views, out, seen, staged, sems):
    blocks, nviews = views.shape[0], views.shape[1]

    @pl.loop(0, out.shape[0])
    def _(peer):
        seen[peer] = 0

    for i in range(blocks):
        for v in range(nviews):
            owner = owners[i, v]
            order = seen[owner]
            seen[owner] = order + 1

            @pl.when(order >= MAIN)
            def _():
                load = pltpu.make_async_copy(views.at[i, v], staged, sems.at[0])
                load.start()
                load.wait()
                store = pltpu.make_async_copy(staged, out.at[owner], sems.at[1])
                store.start()
                store.wait()


def pack_all_thirds(views, owners, peers):
    depth, lat = views.shape[2:]
    return pl.pallas_call(
        all_thirds_kernel,
        out_shape=jax.ShapeDtypeStruct((peers, depth, lat), views.dtype),
        in_specs=[SMEM, ANY],
        out_specs=ANY,
        scratch_shapes=[
            pltpu.SMEM((peers,), jnp.int32),
            pltpu.VMEM((depth, lat), views.dtype),
            pltpu.SemaphoreType.DMA((2,)),
        ],
        name="all_thirds",
    )(owners, views)


def group_count(peers):
    members = 1
    while peers % (2 * members) == 0 and members * members < peers:
        members *= 2
    return peers // members


def along_groups(rows):
    peers = lax.axis_size("join")
    members = peers // len(rows)
    line = [rows[0]]
    for k in range(1, len(rows)):
        line.append(
            lax.ppermute(rows[k], "join", [(i, (i + k * members) % peers) for i in range(peers)])
        )
    return line


def among_members(line):
    peers = lax.axis_size("join")
    members = peers // len(line)
    line = jnp.concatenate(line, axis=0)
    parts = [line]
    for m in range(1, members):
        parts.append(lax.ppermute(line, "join", [(i, i ^ m) for i in range(peers)]))
    return parts


def sources_of_parts(groups):
    peers = lax.axis_size("join")
    members = peers // groups
    here = lax.axis_index("join")
    at = jnp.arange(peers, dtype=jnp.int32)
    group = lax.rem(here // members + groups - lax.rem(at, groups), groups)
    return group * members + jnp.bitwise_xor(lax.rem(here, members), at // groups)


def ends_kernel(start, *refs):
    blocks, out, sems = refs[:-2], refs[-2], refs[-1]
    width = out.shape[1]
    copies, first = [], 0
    for k, block in enumerate(blocks):
        number = block.shape[0]
        copies.append(
            pltpu.make_async_copy(
                block.at[:, pl.ds(pl.multiple_of(start[0], TILE), width)],
                out.at[pl.ds(first, number)],
                sems.at[k],
            )
        )
        first += number
    for copy in copies:
        copy.start()
    for copy in copies:
        copy.wait()


def ends(blocks, start, width):
    if len(blocks) == 1:
        return lax.dynamic_slice_in_dim(blocks[0], start, width, axis=1)
    number = sum(block.shape[0] for block in blocks)
    return pl.pallas_call(
        ends_kernel,
        out_shape=jax.ShapeDtypeStruct((number, width, blocks[0].shape[2]), blocks[0].dtype),
        in_specs=[SMEM] + [ANY] * len(blocks),
        out_specs=ANY,
        scratch_shapes=[pltpu.SemaphoreType.DMA((len(blocks),))],
        name="ends",
    )(jnp.asarray(start, jnp.int32)[None], *blocks)


def halos(blocks, depth, width):
    count = lax.axis_size("view")
    if count == 1:
        return []
    if count == 2:
        sent = ends(blocks, jnp.where(lax.axis_index("view") == 0, depth - width, 0), width)
        return [lax.ppermute(sent, "view", [(0, 1), (1, 0)])]
    forward = [(i, i + 1) for i in range(count - 1)]
    backward = [(target, source) for source, target in forward]
    low = lax.ppermute(ends(blocks, depth - width, width), "view", forward)
    high = lax.ppermute(ends(blocks, 0, width), "view", backward)
    return [low, high]


def framed(block, sides, dim):
    if not sides:
        return block
    if len(sides) == 2:
        return jnp.concatenate([sides[0], block, sides[1]], axis=dim)
    (side,) = sides
    return jnp.where(
        lax.axis_index("view") == 0,
        jnp.concatenate([block, side], axis=dim),
        jnp.concatenate([side, block], axis=dim),
    )


def low_rows():
    count = lax.axis_size("view")
    if count == 2:
        return jnp.where(lax.axis_index("view") == 0, 0, H).astype(jnp.int32)
    return jnp.int32(0 if count == 1 else H)


def halo_rows(sweep):
    return VIEW_HALO - 2 * H * sweep


def piece_starts(depth, sweep):
    count = lax.axis_size("view")
    width = halo_rows(sweep)
    if count == 1:
        return [jnp.int32(0)]
    if count == 2:
        first = lax.axis_index("view") == 0
        return [jnp.where(first, 0, width), jnp.where(first, depth, 0)]
    return [jnp.int32(width), jnp.int32(0), jnp.int32(width + depth)]


def bands_kernel(shapes, shifts, taps_rows, *refs):
    width = taps_rows.shape[-1]
    nviews = taps_rows.shape[1]

    def band(which, v, shift, rows):
        spread = jnp.broadcast_to(taps_rows[which, v : v + 1, :], (rows, width))
        return pltpu.roll(pltpu.roll(spread, 0, 1, stride=1, stride_axis=0), shift, 1)

    at = 0
    for sweep, pieces in enumerate(shapes):
        forward, mirror = refs[2 * sweep], refs[2 * sweep + 1]
        columns, outs = forward.shape[2], mirror.shape[1]
        lane = lax.broadcasted_iota(jnp.int32, (outs, width), 1)
        for v in range(nviews):
            total = jnp.zeros((outs, width), jnp.float32)
            first = 0
            for piece, rows in enumerate(pieces):
                part = band(0, v, shifts[at + 2 * piece], rows)
                forward[v, first : first + rows] = part[:, :columns].astype(forward.dtype)
                inside = jnp.logical_and(lane >= first, lane < first + rows)
                total = jnp.where(inside, band(1, v, shifts[at + 2 * piece + 1], outs), total)
                first += rows
            mirror[v] = total[:, :first].astype(mirror.dtype)
        at += 2 * len(pieces)


def bands(kernel, depth, sides):
    nviews, taps = kernel.shape
    low = low_rows()
    frame = depth + sides * EST_HALO
    width = -(-(frame + 4 * H) // 128) * 128
    shapes, shifts, outs = [], [], []
    for sweep in range(ITERS):
        pieces = (depth,) + (halo_rows(sweep),) * sides
        first = 0
        for rows, start in zip(pieces, piece_starts(depth, sweep)):
            shifts.append(lax.rem(start + low - H + width, width))
            shifts.append(lax.rem(first - start + low - H + width, width))
            first += rows
        shapes.append(pieces)
        rows_in = frame - 2 * sides * H * sweep
        outs.append(jax.ShapeDtypeStruct((nviews, first, rows_in), jnp.bfloat16))
        outs.append(jax.ShapeDtypeStruct((nviews, rows_in - 2 * sides * H, first), jnp.bfloat16))
    rows = jnp.stack([kernel, kernel[:, ::-1]]).astype(jnp.float32)
    rows = jnp.pad(rows, ((0, 0), (0, 0), (0, width - taps)))
    return pl.pallas_call(
        functools.partial(bands_kernel, shapes),
        out_shape=outs,
        in_specs=[SMEM, VMEM],
        out_specs=[VMEM] * len(outs),
        name="bands",
    )(jnp.stack(shifts).astype(jnp.int32), rows)


def plan_kernel(nviews, blocks, here, source, *refs):
    parts, refs = refs[:-11], refs[-11:]
    main_slot, main_code, third_slot, third_source, third_code, numbers, any_crowded = refs[:7]
    tables, rows, scalars, sems = refs[7:]
    per_part, depth, lat = parts[0].shape
    depth -= TILE
    peers = source.shape[0]
    blank = blocks * nviews
    loads = [
        pltpu.make_async_copy(
            part.at[:, pl.ds(depth, TILE)], tables.at[pl.ds(j * per_part, per_part)], sems.at[j]
        )
        for j, part in enumerate(parts)
    ]
    for load in loads:
        load.start()
    for b in range(blocks):
        numbers[2 + b] = 0
    for load in loads:
        load.wait()
    at = lax.broadcasted_iota(jnp.int32, (peers, lat), 0)
    together = jnp.zeros((peers, lat), jnp.float32)
    for t in range(peers):
        row = jnp.broadcast_to(tables[t, :1].astype(jnp.float32), (peers, lat))
        together = jnp.where(at == t, row, together)
    rows[...] = together.astype(jnp.int32)
    copy = pltpu.make_async_copy(rows, scalars, sems.at[len(parts)])
    copy.start()
    copy.wait()

    def enlist(t, carry):
        in_main, in_third, crowded = carry
        for order in range(CAP):
            code = scalars[t, here[0] * CAP + order]
            valid = code >= 0

            @pl.when(valid)
            def _():
                b = code // nviews
                numbers[2 + b] = numbers[2 + b] + 1
                if order < MAIN:
                    main_slot[in_main] = source[t] * MAIN + order
                    main_code[in_main] = code
                else:
                    third_slot[in_third] = t
                    third_source[in_third] = source[t]
                    third_code[in_third] = code

            if order < MAIN:
                in_main = in_main + valid.astype(jnp.int32)
            else:
                in_third = in_third + valid.astype(jnp.int32)
        return in_main, in_third, jnp.maximum(crowded, scalars[t, peers * CAP])

    zero = jnp.int32(0)
    in_main, in_third, crowded = lax.fori_loop(0, peers, enlist, (zero, zero, zero))
    numbers[0] = in_main
    numbers[1] = in_third
    any_crowded[0] = crowded
    for more in range(GROUP - 1):
        main_slot[in_main + more] = main_slot[0]
        main_code[in_main + more] = blank
        third_slot[in_third + more] = third_slot[0]
        third_source[in_third + more] = third_source[0]
        third_code[in_third + more] = blank


def plan(parts, source, here, blocks, nviews):
    peers = source.shape[0]
    lat = parts[0].shape[-1]
    listed = jax.ShapeDtypeStruct((peers * MAIN + GROUP,), jnp.int32)
    thirds = jax.ShapeDtypeStruct((peers + GROUP,), jnp.int32)
    return pl.pallas_call(
        functools.partial(plan_kernel, nviews, blocks),
        out_shape=(listed,) * 2
        + (thirds,) * 3
        + (jax.ShapeDtypeStruct((2 + blocks,), jnp.int32), jax.ShapeDtypeStruct((1,), jnp.int32)),
        in_specs=[SMEM] * 2 + [ANY] * len(parts),
        out_specs=(SMEM,) * 7,
        scratch_shapes=[
            pltpu.VMEM((peers, TILE, lat), parts[0].dtype),
            pltpu.VMEM((peers, lat), jnp.int32),
            pltpu.SMEM((peers, lat), jnp.int32),
            pltpu.SemaphoreType.DMA((len(parts) + 1,)),
        ],
        name="plan",
    )(here[None], source, *parts)


def deconvolve_kernel(nparts, sides, guard, low_ref, *refs):
    main_slot, main_code, third_slot, third_code, numbers = refs[:5]
    main, refs = refs[5], refs[6:]
    parts, refs = refs[:nparts], refs[nparts:]
    main_halo, third_halo, refs = refs[:sides], refs[sides : 2 * sides], refs[2 * sides :]
    est, refs = refs[0], refs[1:]
    bands_of, refs = refs[: 2 * ITERS], refs[2 * ITERS :]
    out, held, recip, following, total, result, sems = refs
    blocks, depth, lat = out.shape
    nviews = bands_of[0].shape[0]
    per_part = parts[0].shape[0]
    low = pl.multiple_of(low_ref[0], H)
    counts = [numbers[2 + b] for b in range(blocks)]
    recip[blocks * nviews] = jnp.zeros(recip.shape[1:], recip.dtype)

    @pl.loop(0, numbers[1])
    def _(p):
        slot = third_slot[p]
        for j, part in enumerate(parts):

            @pl.when(jnp.logical_and(slot >= j * per_part, slot < (j + 1) * per_part))
            def _():
                held[p] = part[slot - j * per_part, :depth]

    stores = []
    for sweep in range(ITERS):
        current = est if sweep == 0 else following
        forward, mirror = bands_of[2 * sweep], bands_of[2 * sweep + 1]
        next_rows, view_rows = mirror.shape[1], mirror.shape[2]
        side_rows = halo_rows(sweep)
        next_at = pl.multiple_of(2 * low, 2 * H)
        halo_at = [pl.multiple_of(2 * sweep * low, 2 * H), 0]
        for b in range(blocks):

            @pl.when(counts[b] > 0)
            def _():
                rounded = current[b].astype(jnp.bfloat16)
                for v in range(nviews):
                    blurred = jnp.dot(forward[v], rounded, preferred_element_type=jnp.float32)
                    inverse = 1.0 / blurred
                    if guard:
                        inverse = jnp.where(blurred > 0, inverse, 0.0)
                    recip[b * nviews + v, :view_rows] = inverse

        total[:, :next_rows] = jnp.zeros((blocks + 1, next_rows, lat), jnp.float32)

        def add(number, held_at, halo, slot_at, code_at):
            @pl.loop(0, (number + (GROUP - 1)) // GROUP)
            def _(group):
                gained = []
                for member in range(GROUP):
                    p = group * GROUP + member
                    code = code_at[p]
                    b = code // nviews
                    pieces = [held_at(p).astype(jnp.float32) * recip[code, :depth]]
                    for side, ref in enumerate(halo):
                        first = depth + side * side_rows
                        rows = ref[slot_at[p], pl.ds(halo_at[side], side_rows)]
                        pieces.append(
                            rows.astype(jnp.float32) * recip[code, first : first + side_rows]
                        )
                    quotient = jnp.concatenate([q.astype(jnp.bfloat16) for q in pieces], axis=0)
                    part = jnp.dot(
                        mirror[code - b * nviews], quotient, preferred_element_type=jnp.float32
                    )
                    gained.append((b, part))
                for b, part in gained:
                    total[b, :next_rows] += part

        add(numbers[0], lambda p: main[main_slot[p]], main_halo, main_slot, main_code)
        add(numbers[1], lambda p: held[p], third_halo, third_slot, third_code)
        for b in range(blocks):

            @pl.when(counts[b] > 0)
            def _():
                updated = current[b, pl.ds(next_at, next_rows)] * (
                    total[b, :next_rows] / counts[b].astype(jnp.float32)
                )
                if sweep < ITERS - 1:
                    following[b] = updated
                else:
                    result[b] = updated

            if sweep == ITERS - 1:

                @pl.when(counts[b] == 0)
                def _():
                    at = pl.multiple_of(2 * ITERS * low, 2 * H)
                    result[b] = est[b, pl.ds(at, depth)]

                store = pltpu.make_async_copy(result.at[b], out.at[b], sems.at[b])
                store.start()
                stores.append(store)
    for store in stores:
        store.wait()


def deconvolve(lists, main, parts, main_halo, third_halo, est, matrices, depth, guard):
    blocks, frame, lat = est.shape
    nviews, view_rows = matrices[0].shape[:2]
    sides = len(main_halo)
    thirds = lists[2].shape[0]
    inputs = [main, *parts, *main_halo, *third_halo, est, *matrices]
    return pl.pallas_call(
        functools.partial(deconvolve_kernel, len(parts), sides, guard),
        out_shape=jax.ShapeDtypeStruct((blocks, depth, lat), jnp.float32),
        in_specs=[SMEM] * (1 + len(lists)) + [VMEM] * len(inputs),
        out_specs=pl.BlockSpec(memory_space=pltpu.HBM),
        scratch_shapes=[
            pltpu.VMEM((thirds, depth, lat), jnp.bfloat16),
            pltpu.VMEM((blocks * nviews + 1, view_rows, lat), jnp.float32),
            pltpu.VMEM((blocks, frame - 2 * sides * H, lat), jnp.float32),
            pltpu.VMEM((blocks + 1, frame - 2 * sides * H, lat), jnp.float32),
            pltpu.VMEM((blocks, depth, lat), jnp.float32),
            pltpu.SemaphoreType.DMA((blocks,)),
        ],
        compiler_params=pltpu.CompilerParams(vmem_limit_bytes=24 * 1024 * 1024),
        name="deconvolve",
    )(low_rows()[None], *lists, *inputs)


def local(estimate, views, owners, local_blocks, psf):
    blocks, depth, lat = estimate.shape
    nviews = views.shape[1]
    peers = lax.axis_size("join")
    groups = group_count(peers)
    here = lax.axis_index("join").astype(jnp.int32)
    normed = psf / jnp.sum(psf, axis=1, keepdims=True)
    kernel = normed.astype(jnp.bfloat16)

    packed, *rows = pack(
        views, owners, local_blocks, (here // (peers // groups))[None], peers, groups
    )
    packed, line = lax.optimization_barrier((packed, along_groups(rows)))
    arrived = lax.all_to_all(
        packed.reshape(peers, MAIN, depth, lat), "join", split_axis=0, concat_axis=0, tiled=True
    ).reshape(peers * MAIN, depth, lat)

    parts = among_members(line)
    source = sources_of_parts(groups)
    est_halos = halos([estimate], depth, EST_HALO)
    est = framed(estimate, est_halos, 1)
    matrices = bands(kernel, depth, len(est_halos))
    parts, source, est, matrices = lax.optimization_barrier((parts, source, est, matrices))
    third_halo = halos(parts, depth, VIEW_HALO)
    lists = plan(parts, source, here, blocks, nviews)
    arrived, parts, third_halo, lists, est, matrices = lax.optimization_barrier(
        (arrived, parts, third_halo, lists, est, matrices)
    )

    main_halo = halos([arrived], depth, VIEW_HALO)
    main_slot, main_code, third_slot, third_source, third_code, numbers, any_crowded = lists
    guard = lax.axis_size("view") > 2

    def finish(third_at, thirds, third_halo):
        return deconvolve(
            (main_slot, main_code, third_at, third_code, numbers),
            arrived,
            thirds,
            main_halo,
            third_halo,
            est,
            matrices,
            depth,
            guard,
        )

    def fallback():
        sent = pack_all_thirds(views, owners, peers)
        thirds = lax.all_to_all(sent, "join", split_axis=0, concat_axis=0, tiled=True)
        return finish(third_source, [thirds], halos([thirds], depth, VIEW_HALO))

    return lax.cond(
        any_crowded[0] > 0, fallback, lambda: finish(third_slot, parts, third_halo)
    )


def solution(mesh):
    in_specs = (
        P("join", "view", None),
        P("join", None, "view", None),
        P("join", None),
        P("join", None),
        P(),
    )
    out_specs = P("join", "view", None)
    return jax.shard_map(local, mesh=mesh, in_specs=in_specs, out_specs=out_specs, check_vma=False)
```

time: 660 us -> 79.1 us (0.12); the launches traced: 650 us -> 77.9 us
  blocking collectives: 245 us -> 0 us
  local copies, waits for them, and re-layouts: 175 us -> 1.59 us
  waiting for transfers between devices: 156 us -> 24.2 us
  matrix products: 40.4 us -> 0 us
  Pallas kernels: 0 us -> 27.7 us
  starting transfers between devices: 30.3 us -> 20.8 us
    all_to_all x3 -> x0, blocking collectives: 245 us -> none  [the longest x1 142 us: local(): lax.all_to_all(outgoing.reshape(peer_count, slot_cap, depth, lat_rows), '...]
    gather x4 -> x0, local copies, waits for them, and re-layouts: 153 us -> none  [toeplitz(): picked = jnp.take(kernel, jnp.clip(offset, 0, taps - 1), axis=1)]
    all_to_all x2 -> x1, waiting for transfers between devices: 155 us -> 6.51 us  [local(): lax.all_to_all(packed.reshape(peers, MAIN, depth, lat), 'join', split_axi...]
    dot_general x12 -> x0, matrix products: 40.4 us -> none  [the longest x2 14.5 us: local(): jnp.einsum('se,ezr->szr', send_full, corr_rows, precision=lax.Precision.H...]
    pallas_call x0 -> x5, Pallas kernels: none -> 27.7 us  [the longest x1 7.58 us: deconvolve(): pl.pallas_call(functools.partial(deconvolve_kernel, len(parts), sides, gu...]
    ppermute x8 -> x9, waiting for transfers between devices: 1.7 us -> 17.7 us  [the longest x3 10.2 us: among_members(): parts.append(lax.ppermute(line, 'join', [(i, i ^ m) for i in range(peers)]))]
    dot_general x2 -> x0, local copies, waits for them, and re-layouts: 9.94 us -> none  [local(): jnp.einsum('se,ezr->szr', send_full, corr_rows, precision=lax.Precision.H...]
    all_to_all x2 -> x1, starting transfers between devices: 11.7 us -> 4.66 us  [local(): lax.all_to_all(packed.reshape(peers, MAIN, depth, lat), 'join', split_axi...]
  transfers between devices with their start and end apart: 10 -> 10, of which waited for: 4 -> 5; matrix products, arithmetic and copies ran while one was open for 24% -> 5% of each run, Pallas kernels for 0% -> 22%
where the time goes in v3:
time: 79.1 us; the launch traced here: 77.9 us
  Pallas kernels  27.7 us (35%)
  waiting for transfers between devices  24.2 us (31%)
  starting transfers between devices  20.8 us (26%)
  other arithmetic  2.96 us (4%)
  local copies, waits for them, and re-layouts  1.59 us (2%)
    ppermute x3, waiting for transfers between devices, among_members(): parts.append(lax.ppermute(line, 'join', [(i, i ^ m) for i in range(peers)]))  10.2 us
    ppermute x3, starting transfers between devices, halos(): return [lax.ppermute(sent, 'view', [(0, 1), (1, 0)])]  9.59 us
    pallas_call x1, Pallas kernels, deconvolve(): pl.pallas_call(functools.partial(deconvolve_kernel, len(parts), sides, gu...  7.58 us
    pallas_call x1, Pallas kernels, ends(): pl.pallas_call(ends_kernel, out_shape=jax.ShapeDtypeStruct((number, width...  7.09 us
    all_to_all x1, waiting for transfers between devices, local(): lax.all_to_all(packed.reshape(peers, MAIN, depth, lat), 'join', split_axi...  6.51 us
    pallas_call x1, Pallas kernels, bands(): pl.pallas_call(functools.partial(bands_kernel, shapes), out_shape=outs, i...  6.06 us
    ppermute x3, waiting for transfers between devices, along_groups(): lax.ppermute(rows[k], 'join', [(i, (i + k * members) % peers) for i in ra...  6.02 us
    all_to_all x1, starting transfers between devices, local(): lax.all_to_all(packed.reshape(peers, MAIN, depth, lat), 'join', split_axi...  4.66 us
  transfers between devices with their start and end apart: 10, of which 5 were waited for; matrix products, arithmetic and copies ran while one was open for 5% of the time, Pallas kernels for 22%

profile of v3, /device:TPU:13, one launch (start us, length us, event | category | flops | bytes accessed | tf_op | source)
XLA Modules:
  0.0 77.9 jit_solution(14880558237813168482)
XLA Ops:
  0.0 3.2 %pack.1 = (bf16[32,128,256]{2,1,0:T(8,128)(2,1)}, bf16[1,144,256]{2,1,0:T(8,128)(2,1)}, bf16[1,144,256]{2,1,0:T(8,128)(2,1)}, bf16[1,144,256]{2,1,0:T(8,128)(2,1)}, bf16[1,144,256]{2,1,0:T(8,128)(2,1)}) custom-call(s32[4,6]{1,0:T(4,128)} %owners.1, s32[4,6]{1,0:T(4,128)} %blocks_of.1, s32[1]{0:T(128)} %bitcast.2.here, bf16[4,6,128,256]{3,2,1,0:T(8,128)(2,1)} %views.1), custom_call_target="tpu_custom_call" | custom-call | tf_op jit(solution)/shard_map/pack/pallas_call | solution.py:103
  3.2 1.4 %collective-permute-start.1 = (bf16[1,144,256]{2,1,0:T(8,128)(2,1)}, bf16[1,144,256]{2,1,0:T(8,128)(2,1)S(1)}, u32[]{:S(2)}, u32[]{:S(2)}) collective-permute-start(bf16[1,144,256]{2,1,0:T(8,128)(2,1)} %get-tuple-element.152), channel_id=1, source_target_pairs={{0,8},{2,10},{4,12},{6,14},{8,16},{10,18},{12,20},{14,22},{16,24},... | collective-permute-start | bytes 221192 | tf_op jit(solution)/shard_map/ppermute | solution.py:175
  4.6 1.1 %collective-permute-start.2 = (bf16[1,144,256]{2,1,0:T(8,128)(2,1)}, bf16[1,144,256]{2,1,0:T(8,128)(2,1)S(1)}, u32[]{:S(2)}, u32[]{:S(2)}) collective-permute-start(bf16[1,144,256]{2,1,0:T(8,128)(2,1)} %get-tuple-element.153), channel_id=1, source_target_pairs={{0,16},{2,18},{4,20},{6,22},{8,24},{10,26},{12,28},{14,30},{16,0},... | collective-permute-start | bytes 221192 | tf_op jit(solution)/shard_map/ppermute | solution.py:175
  5.7 1.4 %collective-permute-start.3 = (bf16[1,144,256]{2,1,0:T(8,128)(2,1)}, bf16[1,144,256]{2,1,0:T(8,128)(2,1)S(1)}, u32[]{:S(2)}, u32[]{:S(2)}) collective-permute-start(bf16[1,144,256]{2,1,0:T(8,128)(2,1)} %get-tuple-element.154), channel_id=1, source_target_pairs={{0,24},{2,26},{4,28},{6,30},{8,0},{10,2},{12,4},{14,6},{16,8},{18,... | collective-permute-start | bytes 221192 | tf_op jit(solution)/shard_map/ppermute | solution.py:175
  7.1 0.0 collective-permute-done.1
  7.1 2.4 %collective-permute-done.2 = bf16[1,144,256]{2,1,0:T(8,128)(2,1)S(1)} collective-permute-done((bf16[1,144,256]{2,1,0:T(8,128)(2,1)}, bf16[1,144,256]{2,1,0:T(8,128)(2,1)S(1)}, u32[]{:S(2)}, u32[]{:S(2)}) %collective-permute-start.2) | collective-permute-done | bytes 73760 | tf_op jit(solution)/shard_map/ppermute | solution.py:175
  9.4 3.7 %collective-permute-done.3 = bf16[1,144,256]{2,1,0:T(8,128)(2,1)S(1)} collective-permute-done((bf16[1,144,256]{2,1,0:T(8,128)(2,1)}, bf16[1,144,256]{2,1,0:T(8,128)(2,1)S(1)}, u32[]{:S(2)}, u32[]{:S(2)}) %collective-permute-start.3) | collective-permute-done | bytes 73760 | tf_op jit(solution)/shard_map/ppermute | solution.py:175
  13.1 0.0 copy-start.1
  13.1 0.0 copy-start.4
  13.1 0.0 copy-start.3
  13.1 4.7 %all-to-all-start.1 = ((bf16[16,2,128,256]{3,2,1,0:T(8,128)(2,1)}), bf16[16,2,128,256]{3,2,1,0:T(8,128)(2,1)S(1)}, u32[]{:S(2)}, u32[]{:S(2)}) async-start(bf16[16,2,128,256]{3,2,1,0:T(8,128)(2,1)} %bitcast.19), calls=%async_computation.1 | async-start | bytes 4194304 | tf_op jit(solution)/shard_map/all_to_all | solution.py:559
  17.8 0.0 copy-done.1
  17.8 2.7 %collective-permute-start.7 = (f32[4,64,256]{2,1,0:T(8,128)S(1)}, f32[4,64,256]{2,1,0:T(8,128)}, u32[]{:S(2)}, u32[]{:S(2)}) collective-permute-start(f32[4,64,256]{2,1,0:T(8,128)S(1)} %constant_dynamic-slice_fusion.2), channel_id=1, source_target_pairs={{0,1},{1,0},{2,3},{3,2},{4,5},{5,4},{6,7},{7,6},{8,9},{9,8},{10,11... | collective-permute-start | bytes 786440 | tf_op jit(solution)/shard_map/ppermute | solution.py:239
  20.5 0.0 copy-done.4
  20.6 0.1 reduce_sum.9
  20.7 0.1 divide_convert_fusion
  20.7 0.1 rev.3
  20.8 0.1 fusion.8
  20.9 0.0 copy-done.3
  21.0 1.2 %collective-permute-start.4 = (bf16[4,144,256]{2,1,0:T(8,128)(2,1)S(1)}, bf16[4,144,256]{2,1,0:T(8,128)(2,1)S(1)}, u32[]{:S(2)}, u32[]{:S(2)}) collective-permute-start(bf16[4,144,256]{2,1,0:T(8,128)(2,1)S(1)} %constant_dynamic-update-slice_fusion.refs_0_), channel_id=1, source_target_pairs={{0,2},{2,0},{4,6},{6,4},{8,10},{10,8},{12,14},{14,12},{16,18},{18,... | collective-permute-start | bytes 884744 | tf_op jit(solution)/shard_map/ppermute | solution.py:186
  22.2 0.3 collective-permute-start.5
  22.5 1.2 %collective-permute-start.6 = (bf16[4,144,256]{2,1,0:T(8,128)(2,1)S(1)}, bf16[4,144,256]{2,1,0:T(8,128)(2,1)}, u32[]{:S(2)}, u32[]{:S(2)}) collective-permute-start(bf16[4,144,256]{2,1,0:T(8,128)(2,1)S(1)} %constant_dynamic-update-slice_fusion.refs_0_), channel_id=1, source_target_pairs={{0,6},{2,4},{4,2},{6,0},{8,14},{10,12},{12,10},{14,8},{16,22},{18,... | collective-permute-start | bytes 884744 | tf_op jit(solution)/shard_map/ppermute | solution.py:186
  23.7 0.6 fusion.3.taps_rows
  24.3 0.6 stack.35.shifts
  24.9 6.1 %bands.1 = (bf16[6,176,192]{2,1,0:T(8,128)(2,1)}, bf16[6,160,176]{2,1,0:T(8,128)(2,1)}, bf16[6,144,160]{2,1,0:T(8,128)(2,1)}, bf16[6,128,144]{2,1,0:T(8,128)(2,1)}) custom-call(s32[8]{0:T(128)} %stack.35.shifts, f32[2,6,256]{2,1,0:T(8,128)} %fusion.3.taps_rows), custom_call_target="tpu_custom_call" | custom-call | tf_op jit(solution)/shard_map/bands/pallas_call | solution.py:327
  31.0 0.5 fusion.5.source
  31.5 0.0 collective-permute-done.7
  31.5 1.5 %maximum_select_fusion = f32[4,192,256]{2,1,0:T(8,128)S(1)} fusion(f32[4,64,256]{2,1,0:T(8,128)} %collective-permute-done.7, f32[4,128,256]{2,1,0:T(8,128)} %param.7, pred[]{:T(512)S(6)} %eq.6), kind=kLoop, calls=%fused_computation.1 | loop fusion | flops 589824 | bytes 1572865 | tf_op jit(solution)/shard_map/jit(_where)/select_n | solution.py:253
  33.0 0.0 collective-permute-done.4.refs_1_
  33.1 10.2 %collective-permute-done.5.refs_2_ = bf16[4,144,256]{2,1,0:T(8,128)(2,1)} collective-permute-done((bf16[4,144,256]{2,1,0:T(8,128)(2,1)S(1)}, bf16[4,144,256]{2,1,0:T(8,128)(2,1)}, u32[]{:S(2)}, u32[]{:S(2)}) %collective-permute-start.5) | collective-permute-done | bytes 294944 | tf_op jit(solution)/shard_map/ppermute | solution.py:186
  43.2 0.0 collective-permute-done.6.refs_3_
  43.2 0.0 copy-start.5
  43.2 7.1 %ends.1 = bf16[16,48,256]{2,1,0:T(8,128)(2,1)} custom-call(s32[1]{0:T(128)} %bitcast.12.start, bf16[4,144,256]{2,1,0:T(8,128)(2,1)S(1)} %constant_dynamic-update-slice_fusion.refs_0_, bf16[4,144,256]{2,1,0:T(8,128)(2,1)S(1)} %collective-permute-done.4.refs_1_, bf16[4,144,256]{2,1,0:T(8,128)(2,1)} %collective-permute-done.5.refs_2_, ...), custom_call_target="tpu_custom_call" | custom-call | tf_op jit(solution)/shard_map/ends/pallas_call | solution.py:223
  50.3 5.3 %collective-permute-start.8 = (bf16[16,48,256]{2,1,0:T(8,128)(2,1)}, bf16[16,48,256]{2,1,0:T(8,128)(2,1)}, u32[]{:S(2)}, u32[]{:S(2)}) collective-permute-start(bf16[16,48,256]{2,1,0:T(8,128)(2,1)} %ends.1), channel_id=1, source_target_pairs={{0,1},{1,0},{2,3},{3,2},{4,5},{5,4},{6,7},{7,6},{8,9},{9,8},{10,11... | collective-permute-start | bytes 1179656 | tf_op jit(solution)/shard_map/ppermute | solution.py:239
  55.6 3.7 %plan.1 = (s32[40]{0:T(128)S(1)}, s32[40]{0:T(128)S(1)}, s32[24]{0:T(128)S(1)}, s32[24]{0:T(128)}, s32[24]{0:T(128)S(1)}, /*index=5*/s32[6]{0:T(128)S(1)}, s32[1]{0:T(128)}) custom-call(s32[1]{0:T(128)} %bitcast.13.here, s32[16]{0:T(128)} %fusion.5.source, bf16[4,144,256]{2,1,0:T(8,128)(2,1)S(1)} %constant_dynamic-update-slice_fusion.refs_0_, ...), custom_call_target="tpu_custom_call" | custom-call | tf_op jit(solution)/shard_map/plan/pallas_call | solution.py:408
  59.4 0.0 collective-permute-done.8
  59.4 6.5 %all-to-all-done.1 = bf16[16,2,128,256]{3,2,1,0:T(8,128)(2,1)S(1)} async-done(((bf16[16,2,128,256]{3,2,1,0:T(8,128)(2,1)}), bf16[16,2,128,256]{3,2,1,0:T(8,128)(2,1)S(1)}, u32[]{:S(2)}, u32[]{:S(2)}) %all-to-all-start.1) | async-done | bytes 2097184 | tf_op jit(solution)/shard_map/all_to_all | solution.py:559
  65.9 0.1 constant_dynamic-slice_fusion.1
  66.0 1.5 %collective-permute-start.9 = (bf16[32,48,256]{2,1,0:T(8,128)(2,1)S(1)}, bf16[32,48,256]{2,1,0:T(8,128)(2,1)}, u32[]{:S(2)}, u32[]{:S(2)}) collective-permute-start(bf16[32,48,256]{2,1,0:T(8,128)(2,1)S(1)} %constant_dynamic-slice_fusion.1), channel_id=1, source_target_pairs={{0,1},{1,0},{2,3},{3,2},{4,5},{5,4},{6,7},{7,6},{8,9},{9,8},{10,11... | collective-permute-start | bytes 2359304 | tf_op jit(solution)/shard_map/ppermute | solution.py:239
  68.1 1.5 %collective-permute-done.9 = bf16[32,48,256]{2,1,0:T(8,128)(2,1)} collective-permute-done((bf16[32,48,256]{2,1,0:T(8,128)(2,1)S(1)}, bf16[32,48,256]{2,1,0:T(8,128)(2,1)}, u32[]{:S(2)}, u32[]{:S(2)}) %collective-permute-start.9) | collective-permute-done | bytes 786464 | tf_op jit(solution)/shard_map/ppermute | solution.py:239
  69.5 0.0 copy-done.5
  69.5 7.6 %conditional.1 = (f32[4,128,256]{2,1,0:T(8,128)S(1)}) conditional(s32[]{:T(128)} %bitcast.14, (s32[40]{0:T(128)S(1)}, s32[40]{0:T(128)S(1)}, s32[24]{0:T(128)S(1)}, s32[24]{0:T(128)S(1)}, s32[6]{0:T(128)S(1)}, /*index=5*/bf16[32,128,256]{2,1,0:T(8,128)(2,1)S(1)}, bf16[4,144,256]{2,1,0:T(8,128)(2,1)S(1)}, bf16[4,144,256]{2,1,0:T(8,128)(2,1)S(1)}, ...), branch_computations={%region_1.2_spmd, %region_2.3_spmd} | conditional | flops 5 | bytes 8651455 | solution.py:597
  69.5 7.6 %deconvolve.2 = f32[4,128,256]{2,1,0:T(8,128)S(1)} custom-call(s32[1]{0:T(128)} %bitcast.low_ref, s32[40]{0:T(128)S(1)} %get-tuple-element.70.refs_0_, s32[40]{0:T(128)S(1)} %get-tuple-element.71.refs_1_, s32[24]{0:T(128)S(1)} %get-tuple-element.72.refs_2_, s32[24]{0:T(128)S(1)} %get-tuple-element.73.refs_3_, s32[6]{0:T(128)S(1)} %get-tuple-element.74.refs_4_, ...), custom_call_target="tpu_custom_call" | custom-call | tf_op jit(solution)/shard_map/cond/branch_0_fun/deconvolve/pallas_call | solution.py:528
  77.1 0.0 copy-start.2
  77.2 0.8 %copy-done.2 = f32[4,128,256]{2,1,0:T(8,128)} copy-done((f32[4,128,256]{2,1,0:T(8,128)}, f32[4,128,256]{2,1,0:T(8,128)S(1)}, u32[]{:S(2)}) %copy-start.2) | copy-done | bytes 524312
  (5 shorter events, 0.1 us)
Async XLA Ops:
  3.2 3.9 %collective-permute-start.1 = (bf16[1,144,256]{2,1,0:T(8,128)(2,1)}, bf16[1,144,256]{2,1,0:T(8,128)(2,1)S(1)}, u32[]{:S(2)}, u32[]{:S(2)}) collective-permute-start(bf16[1,144,256]{2,1,0:T(8,128)(2,1)} %get-tuple-element.152), channel_id=1, source_target_pairs={{0,8},{2,10},{4,12},{6,14},{8,16},{10,18},{12,20},{14,22},{16,24},... | collective-permute-start | bytes 221192 | tf_op jit(solution)/shard_map/ppermute | solution.py:175
  4.6 4.8 %collective-permute-start.2 = (bf16[1,144,256]{2,1,0:T(8,128)(2,1)}, bf16[1,144,256]{2,1,0:T(8,128)(2,1)S(1)}, u32[]{:S(2)}, u32[]{:S(2)}) collective-permute-start(bf16[1,144,256]{2,1,0:T(8,128)(2,1)} %get-tuple-element.153), channel_id=1, source_target_pairs={{0,16},{2,18},{4,20},{6,22},{8,24},{10,26},{12,28},{14,30},{16,0},... | collective-permute-start | bytes 221192 | tf_op jit(solution)/shard_map/ppermute | solution.py:175
  5.7 7.4 %collective-permute-start.3 = (bf16[1,144,256]{2,1,0:T(8,128)(2,1)}, bf16[1,144,256]{2,1,0:T(8,128)(2,1)S(1)}, u32[]{:S(2)}, u32[]{:S(2)}) collective-permute-start(bf16[1,144,256]{2,1,0:T(8,128)(2,1)} %get-tuple-element.154), channel_id=1, source_target_pairs={{0,24},{2,26},{4,28},{6,30},{8,0},{10,2},{12,4},{14,6},{16,8},{18,... | collective-permute-start | bytes 221192 | tf_op jit(solution)/shard_map/ppermute | solution.py:175
  13.1 4.7 %copy-start.1 = (f32[4,128,256]{2,1,0:T(8,128)S(1)}, f32[4,128,256]{2,1,0:T(8,128)}, u32[]{:S(2)}) copy-start(f32[4,128,256]{2,1,0:T(8,128)} %param.7) | copy-start | bytes 1572868
  13.1 7.4 %copy-start.4 = (f32[6,33]{1,0:T(8,128)S(1)}, f32[6,33]{1,0:T(8,128)}, u32[]{:S(2)}) copy-start(f32[6,33]{1,0:T(8,128)} %param.11) | copy-start | bytes 2380
  13.1 7.8 %copy-start.3 = (bf16[1,144,256]{2,1,0:T(8,128)(2,1)S(1)}, bf16[1,144,256]{2,1,0:T(8,128)(2,1)}, u32[]{:S(2)}) copy-start(bf16[1,144,256]{2,1,0:T(8,128)(2,1)} %get-tuple-element.156) | copy-start | bytes 221188
  13.1 52.8 %all-to-all-start.1 = ((bf16[16,2,128,256]{3,2,1,0:T(8,128)(2,1)}), bf16[16,2,128,256]{3,2,1,0:T(8,128)(2,1)S(1)}, u32[]{:S(2)}, u32[]{:S(2)}) async-start(bf16[16,2,128,256]{3,2,1,0:T(8,128)(2,1)} %bitcast.19), calls=%async_computation.1 | async-start | bytes 4194304 | tf_op jit(solution)/shard_map/all_to_all | solution.py:559
  17.8 13.7 %collective-permute-start.7 = (f32[4,64,256]{2,1,0:T(8,128)S(1)}, f32[4,64,256]{2,1,0:T(8,128)}, u32[]{:S(2)}, u32[]{:S(2)}) collective-permute-start(f32[4,64,256]{2,1,0:T(8,128)S(1)} %constant_dynamic-slice_fusion.2), channel_id=1, source_target_pairs={{0,1},{1,0},{2,3},{3,2},{4,5},{5,4},{6,7},{7,6},{8,9},{9,8},{10,11... | collective-permute-start | bytes 786440 | tf_op jit(solution)/shard_map/ppermute | solution.py:239
  21.0 12.1 %collective-permute-start.4 = (bf16[4,144,256]{2,1,0:T(8,128)(2,1)S(1)}, bf16[4,144,256]{2,1,0:T(8,128)(2,1)S(1)}, u32[]{:S(2)}, u32[]{:S(2)}) collective-permute-start(bf16[4,144,256]{2,1,0:T(8,128)(2,1)S(1)} %constant_dynamic-update-slice_fusion.refs_0_), channel_id=1, source_target_pairs={{0,2},{2,0},{4,6},{6,4},{8,10},{10,8},{12,14},{14,12},{16,18},{18,... | collective-permute-start | bytes 884744 | tf_op jit(solution)/shard_map/ppermute | solution.py:186
  22.2 21.0 %collective-permute-start.5 = (bf16[4,144,256]{2,1,0:T(8,128)(2,1)S(1)}, bf16[4,144,256]{2,1,0:T(8,128)(2,1)}, u32[]{:S(2)}, u32[]{:S(2)}) collective-permute-start(bf16[4,144,256]{2,1,0:T(8,128)(2,1)S(1)} %constant_dynamic-update-slice_fusion.refs_0_), channel_id=1, source_target_pairs={{0,4},{2,6},{4,0},{6,2},{8,12},{10,14},{12,8},{14,10},{16,20},{18,... | collective-permute-start | bytes 884744 | tf_op jit(solution)/shard_map/ppermute | solution.py:186
  22.5 20.7 %collective-permute-start.6 = (bf16[4,144,256]{2,1,0:T(8,128)(2,1)S(1)}, bf16[4,144,256]{2,1,0:T(8,128)(2,1)}, u32[]{:S(2)}, u32[]{:S(2)}) collective-permute-start(bf16[4,144,256]{2,1,0:T(8,128)(2,1)S(1)} %constant_dynamic-update-slice_fusion.refs_0_), channel_id=1, source_target_pairs={{0,6},{2,4},{4,2},{6,0},{8,14},{10,12},{12,10},{14,8},{16,22},{18,... | collective-permute-start | bytes 884744 | tf_op jit(solution)/shard_map/ppermute | solution.py:186
  43.2 26.3 %copy-start.5 = (s32[4,6]{1,0:T(4,128)S(1)}, s32[4,6]{1,0:T(4,128)}, u32[]{:S(2)}) copy-start(s32[4,6]{1,0:T(4,128)} %owners.1) | copy-start | bytes 292
  50.3 9.1 %collective-permute-start.8 = (bf16[16,48,256]{2,1,0:T(8,128)(2,1)}, bf16[16,48,256]{2,1,0:T(8,128)(2,1)}, u32[]{:S(2)}, u32[]{:S(2)}) collective-permute-start(bf16[16,48,256]{2,1,0:T(8,128)(2,1)} %ends.1), channel_id=1, source_target_pairs={{0,1},{1,0},{2,3},{3,2},{4,5},{5,4},{6,7},{7,6},{8,9},{9,8},{10,11... | collective-permute-start | bytes 1179656 | tf_op jit(solution)/shard_map/ppermute | solution.py:239
  66.0 3.6 %collective-permute-start.9 = (bf16[32,48,256]{2,1,0:T(8,128)(2,1)S(1)}, bf16[32,48,256]{2,1,0:T(8,128)(2,1)}, u32[]{:S(2)}, u32[]{:S(2)}) collective-permute-start(bf16[32,48,256]{2,1,0:T(8,128)(2,1)S(1)} %constant_dynamic-slice_fusion.1), channel_id=1, source_target_pairs={{0,1},{1,0},{2,3},{3,2},{4,5},{5,4},{6,7},{7,6},{8,9},{9,8},{10,11... | collective-permute-start | bytes 2359304 | tf_op jit(solution)/shard_map/ppermute | solution.py:239
  77.1 0.8 %copy-start.2 = (f32[4,128,256]{2,1,0:T(8,128)}, f32[4,128,256]{2,1,0:T(8,128)S(1)}, u32[]{:S(2)}) copy-start(f32[4,128,256]{2,1,0:T(8,128)S(1)} %get-tuple-element.214) | copy-start | bytes 1572868
